TPU v7x, 512 devices: a whole 4x8x8 slice. The times are simulated.
512 devices in a mesh: seq: 16 (over x_hi, y), group: 32 (over z, x_lo, core).
Axes of the slice: x: 4 (x_hi: 2, x_lo: 2; x = x_hi * 2 + x_lo), y: 8, z: 8, core: 2. Of those that a mesh axis runs over, the one named last changes fastest.
Arguments:
- query_proj: bfloat16 [32, 1024, 8192], P('group', 'seq'), may hold values from -6 to 6
- key_proj: bfloat16 [32, 1024, 1024], P('group', 'seq'), may hold values from -6 to 6
- value_proj: bfloat16 [32, 1024, 1024], P('group', 'seq'), may hold values from -6 to 6
- query_gain: float32 [128], replicated, may hold values from 1 to 5.5, as said below
- key_gain: float32 [128], replicated, may hold values from 1 to 5.5, as said below
- doc_lengths: int32 [32, 4], P('group'), may hold values from 1 to 512, 1024 in all within a row
Outputs:
- attended: bfloat16 [32, 1024, 8192], P('group', 'seq')
- cache: bfloat16 [16, 32, 32, 1, 16, 256], P('seq', 'group')
Inputs may be any that keep to these rules, and one draw needn't show every extreme that they name: `query_gain`: a gain for each of the 128 features. `key_gain`: a gain for each of the 128 features.
All inputs are finite; a program needn't handle non-finite values.
Results may differ from a plain program's by a relative error of at most 0.0045.
The roundings to bfloat16 on the way count: a program that leaves them out, or rounds other values in their place, can miss the bound.
Values may be sent and summed in bfloat16 or wider, within the bound.
No kernel may reach another device: no remote copies, remote signals or barrier semaphores. Data moves between devices by JAX's collectives and lax.ppermute only.
A program may use at most 64 MiB of HBM per device.

v0:
```python
import math

import jax
import jax.numpy as jnp
from jax import lax
from jax.sharding import PartitionSpec as P

PAGE = 16


NORM_EPS = 1e-06
ROPE_BASE = 1000000.0
MASKED = -1e30


def token_starts(lengths, count):
    doc_ends = jnp.cumsum(lengths)
    token_index = jnp.arange(count, dtype=jnp.int32)
    passed = (doc_ends[None, :] <= token_index[:, None]).astype(jnp.int32)
    return jnp.sum(passed * lengths[None, :], axis=1)


def rope_tables(positions, head_width):
    half_width = head_width // 2
    exponent = jnp.arange(half_width, dtype=jnp.float32) * (-2.0 / head_width)
    inverse = jnp.power(jnp.float32(ROPE_BASE), exponent)
    angles = positions.astype(jnp.float32)[:, None] * inverse[None, :]
    return (jnp.cos(angles), jnp.sin(angles))


def norm_rope(heads_in, gain, cosine, sine):
    values_f = heads_in.astype(jnp.float32)
    inv_rms = lax.rsqrt(jnp.mean(values_f * values_f, axis=-1, keepdims=True) + NORM_EPS)
    normed = values_f * inv_rms * gain
    half_width = heads_in.shape[-1] // 2
    front = normed[..., :half_width]
    back_half = normed[..., half_width:]
    cos_b = cosine[:, None, :]
    sin_b = sine[:, None, :]
    rotated = jnp.concatenate(
        [front * cos_b - back_half * sin_b, back_half * cos_b + front * sin_b], axis=-1
    )
    return rotated.astype(jnp.bfloat16)


def attend(q_all, kv_all, starts, head_width):
    token_count = q_all.shape[0]
    entry_count = q_all.shape[1]
    head_count = q_all.shape[2]
    block_size = math.gcd(token_count, 512)
    block_count = token_count // block_size
    score_scale = 1.0 / math.sqrt(head_width)
    block_range = jnp.arange(block_size, dtype=jnp.int32)

    def one_block(block_id):
        q_first = block_id * block_size
        q_block = lax.dynamic_slice_in_dim(q_all, q_first, block_size, 0)
        q_index = q_first + block_range
        q_start = lax.dynamic_slice_in_dim(starts, q_first, block_size, 0)

        def key_step(key_block, carry):
            run_top, denom, accum = carry
            kv_block = lax.dynamic_slice_in_dim(kv_all, key_block * block_size, block_size, 0)
            k_index = key_block * block_size + block_range
            scores = (
                jnp.einsum(
                    "qend,ked->enqk",
                    q_block,
                    kv_block[..., :head_width],
                    preferred_element_type=jnp.float32,
                )
                * score_scale
            )
            visible = (k_index[None, :] <= q_index[:, None]) & (
                k_index[None, :] >= q_start[:, None]
            )
            scores = jnp.where(visible, scores, MASKED)
            new_top = jnp.maximum(run_top, jnp.max(scores, axis=-1))
            factor = jnp.exp(run_top - new_top)
            weights = jnp.where(visible, jnp.exp(scores - new_top[..., None]), 0.0)
            denom = denom * factor + jnp.sum(weights, axis=-1)
            update = jnp.einsum(
                "enqk,ked->enqd",
                weights.astype(jnp.bfloat16),
                kv_block[..., head_width:],
                preferred_element_type=jnp.float32,
            )
            accum = accum * factor[..., None] + update
            return (new_top, denom, accum)

        start_top = jnp.full((entry_count, head_count, block_size), MASKED, jnp.float32)
        start_sum = jnp.zeros((entry_count, head_count, block_size), jnp.float32)
        start_acc = jnp.zeros((entry_count, head_count, block_size, head_width), jnp.float32)
        run_top, denom, accum = lax.fori_loop(
            0, block_id + 1, key_step, (start_top, start_sum, start_acc)
        )
        return (accum / denom[..., None]).astype(jnp.bfloat16).transpose(2, 0, 1, 3)

    blocks = lax.map(one_block, jnp.arange(block_count, dtype=jnp.int32))
    return blocks.reshape(token_count, entry_count, head_count, head_width)


def page_cache(kv_all, entry_first, repeat):
    token_count, entry_count, pair_width = kv_all.shape
    slots = lax.axis_size("group")
    pages = token_count // (PAGE * repeat * slots)
    paged = kv_all.reshape(pages, repeat, slots, PAGE, entry_count, pair_width)
    copy_class = (entry_first + 0) % repeat
    chosen = lax.dynamic_index_in_dim(paged, copy_class, 1, False)
    picked = [chosen[:, :, :, 0, :]]
    outgoing = jnp.stack(picked)[:, None]
    moved = lax.all_to_all(outgoing, "group", split_axis=3, concat_axis=1, tiled=True)
    return moved.reshape(entry_count, 1, slots, pages, PAGE, pair_width)


def body(query_proj, key_proj, value_proj, query_gain, key_gain, doc_lengths):
    seq_count = lax.axis_size("seq")
    head_width = query_gain.shape[0]
    row_count = query_proj.shape[1]
    q_heads = query_proj.shape[2] // head_width
    kv_heads = key_proj.shape[2] // head_width
    token_count = row_count * seq_count
    entries = max(kv_heads, seq_count)
    repeat = entries // kv_heads
    local_entries = entries // seq_count
    sharing = q_heads // entries
    starts = token_starts(doc_lengths[0], token_count)
    first_row = lax.axis_index("seq") * row_count
    own_index = first_row + jnp.arange(row_count, dtype=jnp.int32)
    own_starts = lax.dynamic_slice_in_dim(starts, first_row, row_count, 0)
    cosine, sine = rope_tables(own_index - own_starts, head_width)
    q_rot = norm_rope(
        query_proj[0].reshape(row_count, q_heads, head_width), query_gain, cosine, sine
    )
    k_rot = norm_rope(key_proj[0].reshape(row_count, kv_heads, head_width), key_gain, cosine, sine)
    pairs = jnp.concatenate(
        [k_rot, value_proj[0].reshape(row_count, kv_heads, head_width)], axis=-1
    )
    spread = jnp.repeat(pairs, repeat, axis=1).reshape(
        row_count, seq_count, local_entries, 2 * head_width
    )
    q_split = q_rot.reshape(row_count, seq_count, local_entries, sharing, head_width)
    entry_first = lax.axis_index("seq") * local_entries
    q_got, kv_got = (
        lax.all_to_all(q_split, "seq", split_axis=1, concat_axis=0, tiled=True),
        lax.all_to_all(spread, "seq", split_axis=1, concat_axis=0, tiled=True),
    )
    q_all = q_got.reshape(token_count, local_entries, sharing, head_width)
    kv_all = kv_got.reshape(token_count, local_entries, 2 * head_width)
    mixed = attend(q_all, kv_all, starts, head_width)
    back = lax.all_to_all(
        mixed.reshape(token_count, 1, local_entries, sharing, head_width),
        "seq",
        split_axis=0,
        concat_axis=1,
        tiled=True,
    )
    cache = page_cache(kv_all, entry_first, repeat)
    attended = back.reshape(1, row_count, q_heads * head_width)
    return (attended, cache)


def solution(mesh):
    in_specs = (
        P("group", "seq", None),
        P("group", "seq", None),
        P("group", "seq", None),
        P(),
        P(),
        P("group", None),
    )
    out_specs = (P("group", "seq", None), P("seq", "group", None, None, None, None))
    return jax.shard_map(body, mesh=mesh, in_specs=in_specs, out_specs=out_specs, check_vma=False)
```

profile of v0, /device:TPU:2, one launch (start us, length us, event | category | flops | bytes accessed | tf_op | source)
XLA Modules:
  0.0 150.2 jit_solution(15361947048695826945)
XLA Ops:
  0.7 0.9 reduce-window.8
  1.6 0.9 convert_bitcast_fusion.1
  2.9 0.9 copy.72
  3.8 0.7 select_reduce_fusion
  4.6 0.2 multiply_cosine_fusion
  4.8 0.8 multiply_multiply_fusion.1
  5.6 0.2 subtract_convert_fusion.1
  5.8 0.1 pad_maximum_fusion
  6.0 0.9 broadcast_in_dim.18
  6.8 8.8 %all-to-all-start.1 = ((bf16[64,16,1,256]{3,0,2,1:T(8,128)(2,1)}), bf16[64,16,1,256]{3,0,2,1:T(8,128)(2,1)S(1)}, u32[]{:S(2)}, u32[]{:S(2)}) async-start(bf16[64,16,1,256]{3,0,2,1:T(8,128)(2,1)} %bitcast.22), calls=%async_computation.1 | async-start | bytes 1048576 | tf_op jit(solution)/shard_map/all_to_all | solution.py:146
  15.6 0.1 convert_bitcast_fusion
  15.8 0.4 copy.70
  16.2 0.6 multiply_reduce_fusion
  16.8 0.9 multiply_multiply_fusion
  17.7 0.9 subtract_convert_fusion
  18.6 0.7 copy.55
  19.3 0.7 copy.56
  20.0 1.6 %maximum_bitcast_fusion = bf16[64,16,1,4,128]{4,0,3,2,1:T(8,128)(2,1)} fusion(bf16[64,16,1,4,64]{4,0,3,1,2:T(8,128)(2,1)S(1)} %bitcast.144, bf16[64,16,1,4,64]{4,0,3,1,2:T(8,128)(2,1)S(1)} %bitcast.143), kind=kLoop, calls=%fused_computation.35 | loop fusion | flops 2097152 | bytes 2097152 | tf_op jit(solution)/shard_map/concatenate | solution.py:40
  21.6 11.3 %all-to-all-done.1 = bf16[64,16,1,256]{3,0,2,1:T(8,128)(2,1)S(1)} async-done(((bf16[64,16,1,256]{3,0,2,1:T(8,128)(2,1)}), bf16[64,16,1,256]{3,0,2,1:T(8,128)(2,1)S(1)}, u32[]{:S(2)}, u32[]{:S(2)}) %all-to-all-start.1) | async-done | bytes 524320 | tf_op jit(solution)/shard_map/all_to_all | solution.py:146
  32.8 4.5 %all-to-all-start = ((bf16[64,16,1,4,128]{4,0,3,2,1:T(8,128)(2,1)}), bf16[64,16,1,4,128]{4,0,3,2,1:T(8,128)(2,1)S(1)}, u32[]{:S(2)}, u32[]{:S(2)}) async-start(bf16[64,16,1,4,128]{4,0,3,2,1:T(8,128)(2,1)} %maximum_bitcast_fusion), calls=%async_computation | async-start | bytes 2097152 | tf_op jit(solution)/shard_map/all_to_all | solution.py:145
  37.4 0.7 dynamic-slice_bitcast_fusion.4
  38.1 26.5 %all-to-all-done = bf16[64,16,1,4,128]{4,0,3,2,1:T(8,128)(2,1)S(1)} async-done(((bf16[64,16,1,4,128]{4,0,3,2,1:T(8,128)(2,1)}), bf16[64,16,1,4,128]{4,0,3,2,1:T(8,128)(2,1)S(1)}, u32[]{:S(2)}, u32[]{:S(2)}) %all-to-all-start) | async-done | bytes 1048608 | tf_op jit(solution)/shard_map/all_to_all | solution.py:145
  64.6 12.0 %all-to-all-start.3 = ((bf16[1,1,1,32,16,256]{5,4,2,1,0,3:T(8,128)(2,1)}), bf16[1,1,1,32,16,256]{5,4,2,1,0,3:T(8,128)(2,1)}, u32[]{:S(2)}, u32[]{:S(2)}) async-start(bf16[1,1,1,32,16,256]{5,4,2,1,0,3:T(8,128)(2,1)} %dynamic-slice_bitcast_fusion.4), calls=%async_computation.3 | async-start | bytes 524288 | tf_op jit(solution)/shard_map/all_to_all | solution.py:112
  76.7 32.0 %while.29 = (s32[]{:T(128)}, bf16[2,512,1,4,128]{4,1,0,3,2:T(8,128)(2,1)}, s32[2]{0:T(128)S(1)}, bf16[1024,1,4,128]{3,0,2,1:T(8,128)(2,1)S(1)}, s32[1024]{0:T(10...) while((s32[]{:T(128)}, ...), condition=%wide.region_9.10_spmd.clone.clone, body=%wide.region_4.9_spmd.clone.clone.sunk | while | flops 552344576 | bytes 37137528 | solution.py:99
  76.7 0.6 dynamic_slice.35
  78.8 8.5 %while.30 = (s32[]{:T(128)}, f32[1,4,512]{2,1,0:T(4,128)S(1)}, f32[1,4,512]{2,1,0:T(4,128)S(1)}, f32[1,4,512,128]{3,2,1,0:T(8,128)S(1)}, s32[]{:T(128)}, /*index...) while((s32[]{:T(128)}, f32[1,4,512]{2,1,0:T(4,128)S(1)}, ...), condition=%wide.region_8.8_spmd, body=%wide.region_5.7_spmd.sunk | while | flops 551819776 | bytes 33433844 | solution.py:94
  78.9 0.3 compare_and_fusion.2
  79.2 2.8 %fusion.29 = (f32[4,512]{1,0:T(4,128)S(1)}, f32[512,512,4]{1,0,2:T(8,128)}) fusion(pred[512,512]{0,1:T(8,128)(4,1)S(1)} %compare_and_fusion.2, bf16[512,1,4,128]{3,0,2,1:T(8,128)(2,1)S(1)} %get-tuple-element.354, bf16[1024,1,256]{2,0,1:T(8,128)(2,1)S(1)} %get-tuple-element.353, s32[]{:T(128)S(6)} %select_n.74), kind=kOutput, calls=%fused_computation.3.clone.1 | convolution fusion | flops 271579136 | bytes 5120004 | tf_op jit(solution)/shard_map/while/body/eval_jaxpr/while/body/qend,ked->enqk/dot_general | solution.py:66
  82.0 4.2 %fusion.32 = f32[1,4,512,128]{3,2,1,0:T(8,128)S(1)} fusion(f32[512,512,4]{1,0,2:T(8,128)} %get-tuple-element.313, f32[4,512]{1,0:T(4,128)S(1)} %bitcast.136, pred[512,512]{0,1:T(8,128)(4,1)S(1)} %compare_and_fusion.2, f32[1,4,512,128]{3,2,1,0:T(8,128)S(1)} %get-tuple-element.333, f32[4,512]{1,0:T(4,128)S(1)} %get-tuple-element.314, ...), kind=kOutput, calls=%fused_computation.10.clone.1 | convolution fusion | flops 274202624 | bytes 6701064 | tf_op jit(solution)/shard_map/while/body/eval_jaxpr/while/body/enqk,ked->enqd/dot_general | solution.py:82
  86.2 1.0 fusion.31
  87.3 1.1 bitcast_dynamic-update-slice_fusion.2
  88.5 0.6 dynamic_slice.35
  90.6 16.9 %while.30 = (s32[]{:T(128)}, f32[1,4,512]{2,1,0:T(4,128)S(1)}, f32[1,4,512]{2,1,0:T(4,128)S(1)}, f32[1,4,512,128]{3,2,1,0:T(8,128)S(1)}, s32[]{:T(128)}, /*index...) while((s32[]{:T(128)}, f32[1,4,512]{2,1,0:T(4,128)S(1)}, ...), condition=%wide.region_8.8_spmd, body=%wide.region_5.7_spmd.sunk | while | flops 551819776 | bytes 33433844 | solution.py:94
  90.7 0.3 compare_and_fusion.2
  90.9 2.8 %fusion.29 = (f32[4,512]{1,0:T(4,128)S(1)}, f32[512,512,4]{1,0,2:T(8,128)}) fusion(pred[512,512]{0,1:T(8,128)(4,1)S(1)} %compare_and_fusion.2, bf16[512,1,4,128]{3,0,2,1:T(8,128)(2,1)S(1)} %get-tuple-element.354, bf16[1024,1,256]{2,0,1:T(8,128)(2,1)S(1)} %get-tuple-element.353, s32[]{:T(128)S(6)} %select_n.74), kind=kOutput, calls=%fused_computation.3.clone.1 | convolution fusion | flops 271579136 | bytes 5120004 | tf_op jit(solution)/shard_map/while/body/eval_jaxpr/while/body/qend,ked->enqk/dot_general | solution.py:66
  93.8 4.2 %fusion.32 = f32[1,4,512,128]{3,2,1,0:T(8,128)S(1)} fusion(f32[512,512,4]{1,0,2:T(8,128)} %get-tuple-element.313, f32[4,512]{1,0:T(4,128)S(1)} %bitcast.136, pred[512,512]{0,1:T(8,128)(4,1)S(1)} %compare_and_fusion.2, f32[1,4,512,128]{3,2,1,0:T(8,128)S(1)} %get-tuple-element.333, f32[4,512]{1,0:T(4,128)S(1)} %get-tuple-element.314, ...), kind=kOutput, calls=%fused_computation.10.clone.1 | convolution fusion | flops 274202624 | bytes 6701064 | tf_op jit(solution)/shard_map/while/body/eval_jaxpr/while/body/enqk,ked->enqd/dot_general | solution.py:82
  98.0 1.0 fusion.31
  99.1 0.3 compare_and_fusion.2
  99.4 2.8 %fusion.29 = (f32[4,512]{1,0:T(4,128)S(1)}, f32[512,512,4]{1,0,2:T(8,128)}) fusion(pred[512,512]{0,1:T(8,128)(4,1)S(1)} %compare_and_fusion.2, bf16[512,1,4,128]{3,0,2,1:T(8,128)(2,1)S(1)} %get-tuple-element.354, bf16[1024,1,256]{2,0,1:T(8,128)(2,1)S(1)} %get-tuple-element.353, s32[]{:T(128)S(6)} %select_n.74), kind=kOutput, calls=%fused_computation.3.clone.1 | convolution fusion | flops 271579136 | bytes 5120004 | tf_op jit(solution)/shard_map/while/body/eval_jaxpr/while/body/qend,ked->enqk/dot_general | solution.py:66
  102.2 4.2 %fusion.32 = f32[1,4,512,128]{3,2,1,0:T(8,128)S(1)} fusion(f32[512,512,4]{1,0,2:T(8,128)} %get-tuple-element.313, f32[4,512]{1,0:T(4,128)S(1)} %bitcast.136, pred[512,512]{0,1:T(8,128)(4,1)S(1)} %compare_and_fusion.2, f32[1,4,512,128]{3,2,1,0:T(8,128)S(1)} %get-tuple-element.333, f32[4,512]{1,0:T(4,128)S(1)} %get-tuple-element.314, ...), kind=kOutput, calls=%fused_computation.10.clone.1 | convolution fusion | flops 274202624 | bytes 6701064 | tf_op jit(solution)/shard_map/while/body/eval_jaxpr/while/body/enqk,ked->enqd/dot_general | solution.py:82
  106.5 1.0 fusion.31
  107.6 1.1 bitcast_dynamic-update-slice_fusion.2
  108.7 3.0 %copy.63 = bf16[1024,1,1,4,128]{4,3,2,1,0:T(4,128)(2,1)} copy(bf16[1024,1,1,4,128]{4,0,3,2,1:T(8,128)(2,1)} %bitcast.147) | data formatting | bytes 2097152 | tf_op jit(solution)/shard_map/reshape;reshape | solution.py:152
  111.7 5.2 %all-to-all-start.2 = ((bf16[1024,1,1,4,128]{4,3,2,1,0:T(4,128)(2,1)}), bf16[1024,1,1,4,128]{4,3,2,1,0:T(4,128)(2,1)S(1)}, u32[]{:S(2)}, u32[]{:S(2)}) async-start(bf16[1024,1,1,4,128]{4,3,2,1,0:T(4,128)(2,1)} %copy.63), calls=%async_computation.2 | async-start | bytes 2097152 | tf_op jit(solution)/shard_map/all_to_all | solution.py:151
  117.0 28.9 %all-to-all-done.2 = bf16[1024,1,1,4,128]{4,3,2,1,0:T(4,128)(2,1)S(1)} async-done(((bf16[1024,1,1,4,128]{4,3,2,1,0:T(4,128)(2,1)}), bf16[1024,1,1,4,128]{4,3,2,1,0:T(4,128)(2,1)S(1)}, u32[]{:S(2)}, u32[]{:S(2)}) %all-to-all-start.2) | async-done | bytes 1048608 | tf_op jit(solution)/shard_map/all_to_all | solution.py:151
  146.1 0.8 copy.65
  146.9 1.6 %reshape.193 = bf16[1,64,8192]{2,1,0:T(8,128)(2,1)} reshape(bf16[64,16,1,1,4,128]{5,4,1,0,3,2:T(4,128)(2,1)S(1)} %copy.65) | data formatting | bytes 2097152 | tf_op jit(solution)/shard_map/reshape | solution.py:159
  148.5 1.7 %copy.95 = bf16[1,1,32,1,16,256]{5,4,3,2,1,0:T(8,128)(2,1)} copy(bf16[1,1,32,1,16,256]{5,4,3,2,1,0:T(8,128)(2,1)} %bitcast.33) | data formatting | bytes 524288
  (50 shorter events, 1.3 us)
Async XLA Ops:
  0.6 15.0 %copy-start.1 = (bf16[1,64,8192]{2,1,0:T(8,128)(2,1)S(1)}, bf16[1,64,8192]{2,1,0:T(8,128)(2,1)}, u32[]{:S(2)}) copy-start(bf16[1,64,8192]{2,1,0:T(8,128)(2,1)} %param.10) | copy-start | bytes 3145732
  6.8 26.0 %all-to-all-start.1 = ((bf16[64,16,1,256]{3,0,2,1:T(8,128)(2,1)}), bf16[64,16,1,256]{3,0,2,1:T(8,128)(2,1)S(1)}, u32[]{:S(2)}, u32[]{:S(2)}) async-start(bf16[64,16,1,256]{3,0,2,1:T(8,128)(2,1)} %bitcast.22), calls=%async_computation.1 | async-start | bytes 1048576 | tf_op jit(solution)/shard_map/all_to_all | solution.py:146
  15.6 1.2 copy-start.2
  32.8 31.8 %all-to-all-start = ((bf16[64,16,1,4,128]{4,0,3,2,1:T(8,128)(2,1)}), bf16[64,16,1,4,128]{4,0,3,2,1:T(8,128)(2,1)S(1)}, u32[]{:S(2)}, u32[]{:S(2)}) async-start(bf16[64,16,1,4,128]{4,0,3,2,1:T(8,128)(2,1)} %maximum_bitcast_fusion), calls=%async_computation | async-start | bytes 2097152 | tf_op jit(solution)/shard_map/all_to_all | solution.py:145
  64.6 47.2 %all-to-all-start.3 = ((bf16[1,1,1,32,16,256]{5,4,2,1,0,3:T(8,128)(2,1)}), bf16[1,1,1,32,16,256]{5,4,2,1,0,3:T(8,128)(2,1)}, u32[]{:S(2)}, u32[]{:S(2)}) async-start(bf16[1,1,1,32,16,256]{5,4,2,1,0,3:T(8,128)(2,1)} %dynamic-slice_bitcast_fusion.4), calls=%async_computation.3 | async-start | bytes 524288 | tf_op jit(solution)/shard_map/all_to_all | solution.py:112
  82.0 4.3 %copy-start = (f32[512,512,4]{1,0,2:T(8,128)S(1)}, f32[512,512,4]{1,0,2:T(8,128)}, u32[]{:S(2)}) copy-start(f32[512,512,4]{1,0,2:T(8,128)} %get-tuple-element.313) | copy-start | bytes 12582916 | tf_op jit(solution)/shard_map/while/body/eval_jaxpr/while
  93.7 4.3 %copy-start = (f32[512,512,4]{1,0,2:T(8,128)S(1)}, f32[512,512,4]{1,0,2:T(8,128)}, u32[]{:S(2)}) copy-start(f32[512,512,4]{1,0,2:T(8,128)} %get-tuple-element.313) | copy-start | bytes 12582916 | tf_op jit(solution)/shard_map/while/body/eval_jaxpr/while
  102.2 4.3 %copy-start = (f32[512,512,4]{1,0,2:T(8,128)S(1)}, f32[512,512,4]{1,0,2:T(8,128)}, u32[]{:S(2)}) copy-start(f32[512,512,4]{1,0,2:T(8,128)} %get-tuple-element.313) | copy-start | bytes 12582916 | tf_op jit(solution)/shard_map/while/body/eval_jaxpr/while
  111.7 34.2 %all-to-all-start.2 = ((bf16[1024,1,1,4,128]{4,3,2,1,0:T(4,128)(2,1)}), bf16[1024,1,1,4,128]{4,3,2,1,0:T(4,128)(2,1)S(1)}, u32[]{:S(2)}, u32[]{:S(2)}) async-start(bf16[1024,1,1,4,128]{4,3,2,1,0:T(4,128)(2,1)} %copy.63), calls=%async_computation.2 | async-start | bytes 2097152 | tf_op jit(solution)/shard_map/all_to_all | solution.py:151
where the time goes:
time: 151 us; the launch traced here: 150 us
  waiting for transfers between devices  66.7 us (44%)
  starting transfers between devices  30.6 us (20%)
  matrix products  21.1 us (14%)
  other arithmetic  14.6 us (10%)
  local copies, waits for them, and re-layouts  13.5 us (9%)
  loops' own time  2.91 us (2%)
    all_to_all x1, waiting for transfers between devices, body(): lax.all_to_all(mixed.reshape(token_count, 1, local_entries, sharing, head...  28.9 us
    all_to_all x1, waiting for transfers between devices, body(): lax.all_to_all(q_split, 'seq', split_axis=1, concat_axis=0, tiled=True)  26.5 us
    dot_general x3, matrix products, key_step(): jnp.einsum('enqk,ked->enqd', weights.astype(jnp.bfloat16), kv_block[...,...  12.7 us
    all_to_all x1, starting transfers between devices, page_cache(): lax.all_to_all(outgoing, 'group', split_axis=3, concat_axis=1, tiled=True)  12 us
    all_to_all x1, waiting for transfers between devices, body(): lax.all_to_all(spread, 'seq', split_axis=1, concat_axis=0, tiled=True)  11.3 us
    all_to_all x1, starting transfers between devices, body(): lax.all_to_all(spread, 'seq', split_axis=1, concat_axis=0, tiled=True)  8.77 us
    dot_general x3, matrix products, key_step(): jnp.einsum('qend,ked->enqk', q_block, kv_block[..., :head_width], preferr...  8.42 us
    all_to_all x1, starting transfers between devices, body(): lax.all_to_all(mixed.reshape(token_count, 1, local_entries, sharing, head...  5.24 us
  transfers between devices with their start and end apart: 4, of which 3 were waited for; matrix products, arithmetic and copies ran while one was open for 26% of the time, Pallas kernels for 0%

commit v1 on v0

v1 whole, which is shorter than its diff:
```python
import math

import jax
import jax.numpy as jnp
from jax import lax
from jax.experimental import pallas as pl
from jax.experimental.pallas import tpu as pltpu
from jax.sharding import PartitionSpec as P

PAGE = 16
NORM_EPS = 1e-06
ROPE_BASE = 1000000.0
MASKED = -1e30
HD = 128
KVH = 8
SHARE = 8
ROWS = 64
REACH = 8
LOG2E = 1.4426950408889634
VMEM_LIMIT = 40 * 1024 * 1024


def doc_starts(lens_ref, token):
    start = jnp.zeros(token.shape, jnp.int32)
    end = jnp.int32(0)
    for d in range(lens_ref.shape[1]):
        length = lens_ref[0, d]
        end = end + length
        start = start + jnp.where(end <= token, length, 0)
    return start


def inverse_frequency(pair):
    return jnp.exp(pair.astype(jnp.float32) * (-2.0 * math.log(ROPE_BASE) / HD))


def key_kernel(
    where_ref, lens_ref, key_hbm, value_hbm, gain_hbm, kv_ref, key_ref, value_ref, gain_ref, sems
):
    copies = [
        pltpu.make_async_copy(key_hbm.at[0], key_ref, sems.at[0]),
        pltpu.make_async_copy(gain_hbm, gain_ref, sems.at[1]),
        pltpu.make_async_copy(value_hbm.at[0], value_ref, sems.at[2]),
    ]
    for copy in copies:
        copy.start()
    token = where_ref[0] * ROWS + lax.broadcasted_iota(jnp.int32, (ROWS, HD), 0)
    lane = lax.broadcasted_iota(jnp.int32, (ROWS, HD), 1)
    position = token - doc_starts(lens_ref, token)
    half = HD // 2
    angles = position.astype(jnp.float32) * inverse_frequency(
        jnp.where(lane < half, lane, lane - half)
    )
    cosine = jnp.cos(angles)
    sine = jnp.sin(angles)
    sine = jnp.where(lane < half, -sine, sine)
    copies[0].wait()
    copies[1].wait()
    gain = gain_ref[...]
    for h in range(KVH):
        values_f = key_ref[:, pl.ds(h * HD, HD)].astype(jnp.float32)
        inv_rms = lax.rsqrt(jnp.mean(values_f * values_f, axis=-1, keepdims=True) + NORM_EPS)
        normed = values_f * inv_rms * gain
        swapped = pltpu.roll(normed, half, 1)
        kv_ref[h, :, :HD] = (normed * cosine + swapped * sine).astype(jnp.bfloat16)
    copies[2].wait()
    for h in range(KVH):
        kv_ref[h, :, HD:] = value_ref[:, pl.ds(h * HD, HD)]


SMEM_SPEC = pl.BlockSpec(memory_space=pltpu.SMEM)
VMEM_SPEC = pl.BlockSpec(memory_space=pltpu.VMEM)
HBM_SPEC = pl.BlockSpec(memory_space=pltpu.HBM)
PARAMS = pltpu.CompilerParams(vmem_limit_bytes=VMEM_LIMIT)


def stay(array):
    return pltpu.with_memory_space_constraint(array, pltpu.HBM)


def prepare_keys(where, lens, key, value, gain):
    return pl.pallas_call(
        key_kernel,
        out_shape=jax.ShapeDtypeStruct((KVH, ROWS, 2 * HD), jnp.bfloat16),
        in_specs=[SMEM_SPEC, SMEM_SPEC, HBM_SPEC, HBM_SPEC, HBM_SPEC],
        out_specs=VMEM_SPEC,
        scratch_shapes=[
            pltpu.VMEM((ROWS, KVH * HD), jnp.bfloat16),
            pltpu.VMEM((ROWS, KVH * HD), jnp.bfloat16),
            pltpu.VMEM((1, HD), jnp.float32),
            pltpu.SemaphoreType.DMA((3,)),
        ],
        compiler_params=PARAMS,
        name="prepare_keys",
    )(where, lens, stay(key), stay(value), stay(gain))


def query_kernel(where_ref, lens_ref, query_hbm, gain_ref, out_ref, query_ref, sems):
    def copy_of(h):
        piece = pl.ds(h * SHARE * HD, SHARE * HD)
        return pltpu.make_async_copy(
            query_hbm.at[0, :, piece], query_ref.at[:, piece], sems.at[h]
        )

    for h in range(KVH):
        copy_of(h).start()
    half = HD // 2
    lane = lax.broadcasted_iota(jnp.int32, (half, 2 * ROWS), 1)
    token = where_ref[0] * ROWS + jnp.where(lane < ROWS, lane, lane - ROWS)
    position = token - doc_starts(lens_ref, token)
    pair = lax.broadcasted_iota(jnp.int32, (half, 2 * ROWS), 0)
    angles = position.astype(jnp.float32) * inverse_frequency(pair)
    cosine = jnp.cos(angles)
    sine = jnp.sin(angles)
    gain = jnp.broadcast_to(gain_ref[...], (HD, HD)).T
    for h in range(KVH):
        copy_of(h).wait()
        for c in range(SHARE // 2):
            column = (h * SHARE + 2 * c) * HD
            both = jnp.concatenate(
                [query_ref[:, pl.ds(column, HD)], query_ref[:, pl.ds(column + HD, HD)]], axis=0
            )
            values_f = both.T.astype(jnp.float32)
            inv_rms = lax.rsqrt(jnp.mean(values_f * values_f, axis=0, keepdims=True) + NORM_EPS)
            normed = values_f * inv_rms * gain
            front, back = normed[:half], normed[half:]
            lanes = pl.ds(c * 2 * ROWS, 2 * ROWS)
            out_ref[h, :half, lanes] = (front * cosine - back * sine).astype(jnp.bfloat16)
            out_ref[h, half:, lanes] = (back * cosine + front * sine).astype(jnp.bfloat16)


def prepare_queries(where, lens, query, gain):
    return pl.pallas_call(
        query_kernel,
        out_shape=jax.ShapeDtypeStruct((KVH, HD, SHARE * ROWS), jnp.bfloat16),
        in_specs=[SMEM_SPEC, SMEM_SPEC, HBM_SPEC, VMEM_SPEC],
        out_specs=VMEM_SPEC,
        scratch_shapes=[
            pltpu.VMEM((ROWS, KVH * SHARE * HD), jnp.bfloat16),
            pltpu.SemaphoreType.DMA((KVH,)),
        ],
        compiler_params=PARAMS,
        cost_estimate=pl.CostEstimate(flops=10_000_000, bytes_accessed=4 << 20, transcendentals=0),
        name="prepare_queries",
    )(where, lens, stay(query), gain)


def visible_bias(where_ref, lens_ref, offsets):
    shape = (ROWS, 2 * ROWS)
    block = where_ref[0]
    lane = lax.broadcasted_iota(jnp.int32, shape, 1)
    token = block * ROWS + jnp.where(lane < ROWS, lane, lane - ROWS)
    start = doc_starts(lens_ref, token)
    row = lax.broadcasted_iota(jnp.int32, shape, 0)
    pieces = []
    for offset in offsets:
        source = (block - offset) * ROWS + row
        seen = (source >= start) & (source <= token)
        pieces.append(jnp.where(seen, 0.0, MASKED))
    return jnp.concatenate(pieces, axis=0)


def masked_scores(h, query_ref, blocks, bias):
    keys = jnp.concatenate([b[h, :, :HD] for b in blocks], axis=0)
    scores = jnp.dot(keys, query_ref[h], preferred_element_type=jnp.float32)
    return scores * (LOG2E / math.sqrt(HD)) + jnp.concatenate([bias] * (SHARE // 2), axis=1)


def mix_values(h, blocks, weights):
    values = jnp.concatenate([b[h, :, HD:] for b in blocks], axis=0)
    return lax.dot_general(
        values,
        weights.astype(jnp.bfloat16),
        (((0,), (0,)), ((), ())),
        preferred_element_type=jnp.float32,
    )


def early_kernel(offsets, where_ref, lens_ref, query_ref, *refs):
    blocks, (acc_ref, stat_ref) = refs[: len(offsets)], refs[len(offsets) :]
    bias = visible_bias(where_ref, lens_ref, offsets)
    for h in range(KVH):
        scores = masked_scores(h, query_ref, blocks, bias)
        top = jnp.max(scores, axis=0, keepdims=True)
        weights = jnp.exp2(scores - top)
        stat_ref[h, 0:1, :] = top
        stat_ref[h, 1:2, :] = jnp.sum(weights, axis=0, keepdims=True)
        acc_ref[h] = mix_values(h, blocks, weights)


def late_kernel(offsets, where_ref, lens_ref, query_ref, acc_ref, stat_ref, *refs):
    blocks, (out_hbm, out_ref, sems) = refs[: len(offsets)], refs[len(offsets) :]
    bias = visible_bias(where_ref, lens_ref, offsets)
    copies = []
    for h in range(KVH):
        scores = masked_scores(h, query_ref, blocks, bias)
        old_top = stat_ref[h, 0:1, :]
        top = jnp.maximum(old_top, jnp.max(scores, axis=0, keepdims=True))
        keep = jnp.exp2(old_top - top)
        weights = jnp.exp2(scores - top)
        denom = stat_ref[h, 1:2, :] * keep + jnp.sum(weights, axis=0, keepdims=True)
        mixed = (acc_ref[h] * keep + mix_values(h, blocks, weights)) / denom
        rounded = mixed.astype(jnp.bfloat16)
        for c in range(SHARE // 2):
            both = rounded[:, c * 2 * ROWS : (c + 1) * 2 * ROWS].T
            column = (h * SHARE + 2 * c) * HD
            out_ref[:, pl.ds(column, HD)] = both[:ROWS]
            out_ref[:, pl.ds(column + HD, HD)] = both[ROWS:]
        piece = pl.ds(h * SHARE * HD, SHARE * HD)
        copies.append(
            pltpu.make_async_copy(out_ref.at[:, piece], out_hbm.at[0, :, piece], sems.at[h])
        )
        copies[-1].start()
    for copy in copies:
        copy.wait()


def attention_cost(count):
    return pl.CostEstimate(
        flops=4 * KVH * SHARE * ROWS * ROWS * HD * count,
        bytes_accessed=4 << 20,
        transcendentals=KVH * SHARE * ROWS * ROWS * count,
    )


def attend_early(offsets, where, lens, query, blocks):
    count = len(offsets)
    return pl.pallas_call(
        lambda *refs: early_kernel(offsets, *refs),
        out_shape=(
            jax.ShapeDtypeStruct((KVH, HD, SHARE * ROWS), jnp.float32),
            jax.ShapeDtypeStruct((KVH, 8, SHARE * ROWS), jnp.float32),
        ),
        in_specs=[SMEM_SPEC, SMEM_SPEC] + [VMEM_SPEC] * (1 + count),
        out_specs=(VMEM_SPEC, VMEM_SPEC),
        compiler_params=PARAMS,
        cost_estimate=attention_cost(count),
        name="attend_early",
    )(where, lens, query, *blocks)


def attend_late(offsets, where, lens, query, acc, stat, blocks):
    count = len(offsets)
    return pl.pallas_call(
        lambda *refs: late_kernel(offsets, *refs),
        out_shape=jax.ShapeDtypeStruct((1, ROWS, KVH * SHARE * HD), jnp.bfloat16),
        in_specs=[SMEM_SPEC, SMEM_SPEC] + [VMEM_SPEC] * (3 + count),
        out_specs=HBM_SPEC,
        scratch_shapes=[
            pltpu.VMEM((ROWS, KVH * SHARE * HD), jnp.bfloat16),
            pltpu.SemaphoreType.DMA((KVH,)),
        ],
        compiler_params=PARAMS,
        cost_estimate=attention_cost(count),
        name="attend_late",
    )(where, lens, query, acc, stat, *blocks)


def plus_pairs(count, step):
    return [(i, i + 1) for i in range(count - 1) if i + 1 >= step]


def cross_pairs(count):
    return [(i, i + REACH) for i in range(REACH)] + [(REACH + i, i) for i in range(3)]


def minus_pairs(count, step):
    receivers = list(range(REACH - step, count)) + list(range(0, 3 - step))
    return [((r + 1) % count, r) for r in receivers]


def slot_pairs(seqs, groups):
    pairs = []
    spread = groups // KVH
    for s in range(seqs):
        repeat, place = divmod(s, KVH)
        for g in range(groups):
            head, page = divmod(g, spread)
            entry = head * 2 + repeat
            pairs.append((s * groups + g, entry * groups + place * spread + page))
    return pairs


def body(query_proj, key_proj, value_proj, query_gain, key_gain, doc_lengths):
    seqs = lax.axis_size("seq")
    groups = lax.axis_size("group")
    where = lax.axis_index("seq").astype(jnp.int32).reshape(1)
    kv = prepare_keys(where, doc_lengths, key_proj, value_proj, key_gain.reshape(1, HD))
    plus = [lax.ppermute(kv, "seq", plus_pairs(seqs, 1))]
    minus = [lax.ppermute(kv, "seq", cross_pairs(seqs))]
    for step in (2, 3, 4):
        plus.append(lax.ppermute(plus[-1], "seq", plus_pairs(seqs, step)))
        minus.append(lax.ppermute(minus[-1], "seq", minus_pairs(seqs, step - 1)))
    query = prepare_queries(where, doc_lengths, query_proj, query_gain.reshape(1, HD))
    pages = kv.reshape(KVH * (ROWS // PAGE), PAGE, 2 * HD)
    mine = lax.all_to_all(pages, "group", split_axis=0, concat_axis=0, tiled=True)
    cache = lax.ppermute(mine, ("seq", "group"), slot_pairs(seqs, groups))
    acc, stat = attend_early(
        (0, 1, 2, 3, 8, 7, 6), where, doc_lengths, query, [kv] + plus[:3] + minus[:3]
    )
    attended = attend_late((4, 5), where, doc_lengths, query, acc, stat, [plus[3], minus[3]])
    return attended, cache.reshape(1, 1, groups, 1, PAGE, 2 * HD)


def solution(mesh):
    in_specs = (
        P("group", "seq", None),
        P("group", "seq", None),
        P("group", "seq", None),
        P(),
        P(),
        P("group", None),
    )
    out_specs = (P("seq", "group", None, None, None, None),)
    out_specs = (P("group", "seq", None),) + out_specs
    return jax.shard_map(body, mesh=mesh, in_specs=in_specs, out_specs=out_specs, check_vma=False)
```

time: 151 us -> 89.4 us (0.59)
  the two profiles are of different devices: /device:TPU:2 before, /device:TPU:198 now
where the time goes in v1:
time: 89.4 us; the launch traced here: 88.9 us
  starting transfers between devices  47.1 us (53%)
  waiting for transfers between devices  24.6 us (28%)
  Pallas kernels  13.8 us (15%)
  local copies, waits for them, and re-layouts  2.66 us (3%)
    ppermute x3, starting transfers between devices, body(): minus.append(lax.ppermute(minus[-1], 'seq', minus_pairs(seqs, step - 1)))  21.5 us
    ppermute x3, waiting for transfers between devices, body(): minus.append(lax.ppermute(minus[-1], 'seq', minus_pairs(seqs, step - 1)))  18.2 us
    all_to_all x1, starting transfers between devices, body(): lax.all_to_all(pages, 'group', split_axis=0, concat_axis=0, tiled=True)  9.22 us
    ppermute x3, starting transfers between devices, body(): plus.append(lax.ppermute(plus[-1], 'seq', plus_pairs(seqs, step)))  7.29 us
    ppermute x3, waiting for transfers between devices, body(): plus.append(lax.ppermute(plus[-1], 'seq', plus_pairs(seqs, step)))  6.38 us
    pallas_call x1, Pallas kernels, attend_early(): pl.pallas_call(lambda *refs: early_kernel(offsets, *refs), out_shape=(jax...  4.61 us
    pallas_call x1, Pallas kernels, attend_late(): pl.pallas_call(lambda *refs: late_kernel(offsets, *refs), out_shape=jax.S...  3.58 us
    ppermute x1, starting transfers between devices, body(): plus = [lax.ppermute(kv, 'seq', plus_pairs(seqs, 1))]  3.48 us
  transfers between devices with their start and end apart: 10, of which 3 were waited for; matrix products, arithmetic and copies ran while one was open for 0% of the time, Pallas kernels for 8%

profile of v1, /device:TPU:198, one launch (start us, length us, event | category | flops | bytes accessed | tf_op | source)
XLA Modules:
  0.0 88.9 jit_solution(12710064039344104036)
XLA Ops:
  0.6 0.0 copy-start
  0.6 0.6 copy-done
  1.3 2.7 %prepare_keys.1.refs_3_ = bf16[8,64,256]{2,1,0:T(8,128)(2,1)} custom-call(s32[1]{0:T(128)} %bitcast.where_ref.refs_0_, s32[1,4]{1,0:T(1,128)S(1)} %copy-done, bf16[1,64,1024]{2,1,0:T(8,128)(2,1)} %key_hbm.1, bf16[1,64,1024]{2,1,0:T(8,128)(2,1)} %value_hbm.1, f32[1,128]{1,0:T(1,128)} %bitcast.7), custom_call_target="tpu_custom_call" | custom-call | tf_op jit(solution)/shard_map/prepare_keys/pallas_call | solution.py:82
  4.0 3.5 %collective-permute-start = (bf16[8,64,256]{2,1,0:T(8,128)(2,1)}, bf16[8,64,256]{2,1,0:T(8,128)(2,1)S(1)}, u32[]{:S(2)}, u32[]{:S(2)}) collective-permute-start(bf16[8,64,256]{2,1,0:T(8,128)(2,1)} %prepare_keys.1.refs_3_), channel_id=1, source_target_pairs={{0,32},{32,64},{64,96},{96,128},{128,160},{160,192},{192,224},{224... | collective-permute-start | bytes 786440 | tf_op jit(solution)/shard_map/ppermute | solution.py:289
  7.5 3.3 %collective-permute-start.3 = (bf16[8,64,256]{2,1,0:T(8,128)(2,1)}, bf16[8,64,256]{2,1,0:T(8,128)(2,1)S(1)}, u32[]{:S(2)}, u32[]{:S(2)}) collective-permute-start(bf16[8,64,256]{2,1,0:T(8,128)(2,1)} %prepare_keys.1.refs_3_), channel_id=1, source_target_pairs={{0,256},{32,288},{64,320},{96,352},{128,384},{160,416},{192,448},{... | collective-permute-start | bytes 786440 | tf_op jit(solution)/shard_map/ppermute | solution.py:290
  10.9 9.2 %all-to-all-start = ((bf16[32,16,256]{2,1,0:T(8,128)(2,1)}), bf16[32,16,256]{2,1,0:T(8,128)(2,1)S(1)}, u32[]{:S(2)}, u32[]{:S(2)}) async-start(bf16[32,16,256]{2,1,0:T(8,128)(2,1)} %bitcast.3), calls=%async_computation | async-start | bytes 524288 | tf_op jit(solution)/shard_map/all_to_all | solution.py:296
  20.1 0.0 collective-permute-done.refs_4_
  20.1 3.5 %collective-permute-start.1 = (bf16[8,64,256]{2,1,0:T(8,128)(2,1)S(1)}, bf16[8,64,256]{2,1,0:T(8,128)(2,1)S(1)}, u32[]{:S(2)}, u32[]{:S(2)}) collective-permute-start(bf16[8,64,256]{2,1,0:T(8,128)(2,1)S(1)} %collective-permute-done.refs_4_), channel_id=1, source_target_pairs={{32,64},{64,96},{96,128},{128,160},{160,192},{192,224},{224,256},{... | collective-permute-start | bytes 786440 | tf_op jit(solution)/shard_map/ppermute | solution.py:292
  23.6 0.0 collective-permute-done.3.refs_7_
  23.6 6.0 %collective-permute-start.4 = (bf16[8,64,256]{2,1,0:T(8,128)(2,1)S(1)}, bf16[8,64,256]{2,1,0:T(8,128)(2,1)S(1)}, u32[]{:S(2)}, u32[]{:S(2)}) collective-permute-start(bf16[8,64,256]{2,1,0:T(8,128)(2,1)S(1)} %collective-permute-done.3.refs_7_), channel_id=1, source_target_pairs={{256,224},{288,256},{320,288},{352,320},{384,352},{416,384},{448,4... | collective-permute-start | bytes 786440 | tf_op jit(solution)/shard_map/ppermute | solution.py:293
  29.6 5.2 %collective-permute-done.1.refs_5_ = bf16[8,64,256]{2,1,0:T(8,128)(2,1)S(1)} collective-permute-done((bf16[8,64,256]{2,1,0:T(8,128)(2,1)S(1)}, bf16[8,64,256]{2,1,0:T(8,128)(2,1)S(1)}, u32[]{:S(2)}, u32[]{:S(2)}) %collective-permute-start.1) | collective-permute-done | bytes 262176 | tf_op jit(solution)/shard_map/ppermute | solution.py:292
  34.8 1.9 %collective-permute-start.2 = (bf16[8,64,256]{2,1,0:T(8,128)(2,1)S(1)}, bf16[8,64,256]{2,1,0:T(8,128)(2,1)S(1)}, u32[]{:S(2)}, u32[]{:S(2)}) collective-permute-start(bf16[8,64,256]{2,1,0:T(8,128)(2,1)S(1)} %collective-permute-done.1.refs_5_), channel_id=1, source_target_pairs={{64,96},{96,128},{128,160},{160,192},{192,224},{224,256},{256,288}... | collective-permute-start | bytes 786440 | tf_op jit(solution)/shard_map/ppermute | solution.py:292
  36.7 0.0 collective-permute-done.4.refs_8_
  36.7 7.5 %collective-permute-start.5 = (bf16[8,64,256]{2,1,0:T(8,128)(2,1)S(1)}, bf16[8,64,256]{2,1,0:T(8,128)(2,1)S(1)}, u32[]{:S(2)}, u32[]{:S(2)}) collective-permute-start(bf16[8,64,256]{2,1,0:T(8,128)(2,1)S(1)} %collective-permute-done.4.refs_8_), channel_id=1, source_target_pairs={{224,192},{256,224},{288,256},{320,288},{352,320},{384,352},{416,3... | collective-permute-start | bytes 786440 | tf_op jit(solution)/shard_map/ppermute | solution.py:293
  44.2 0.0 all-to-all-done
  44.2 2.3 %collective-permute-start.8 = (bf16[32,16,256]{2,1,0:T(8,128)(2,1)S(1)}, bf16[32,16,256]{2,1,0:T(8,128)(2,1)S(1)}, u32[]{:S(2)}, u32[]{:S(2)}) collective-permute-start(bf16[32,16,256]{2,1,0:T(8,128)(2,1)S(1)} %all-to-all-done), channel_id=1, source_target_pairs={{0,0},{1,1},{2,2},{3,3},{4,64},{5,65},{6,66},{7,67},{8,128},{9,129... | collective-permute-start | bytes 786440 | tf_op jit(solution)/shard_map/ppermute | solution.py:297
  46.5 1.2 %collective-permute-done.2.refs_6_ = bf16[8,64,256]{2,1,0:T(8,128)(2,1)S(1)} collective-permute-done((bf16[8,64,256]{2,1,0:T(8,128)(2,1)S(1)}, bf16[8,64,256]{2,1,0:T(8,128)(2,1)S(1)}, u32[]{:S(2)}, u32[]{:S(2)}) %collective-permute-start.2) | collective-permute-done | bytes 262176 | tf_op jit(solution)/shard_map/ppermute | solution.py:292
  47.7 1.9 %collective-permute-start.6 = (bf16[8,64,256]{2,1,0:T(8,128)(2,1)S(1)}, bf16[8,64,256]{2,1,0:T(8,128)(2,1)S(1)}, u32[]{:S(2)}, u32[]{:S(2)}) collective-permute-start(bf16[8,64,256]{2,1,0:T(8,128)(2,1)S(1)} %collective-permute-done.2.refs_6_), channel_id=1, source_target_pairs={{96,128},{128,160},{160,192},{192,224},{224,256},{256,288},{288,32... | collective-permute-start | bytes 786440 | tf_op jit(solution)/shard_map/ppermute | solution.py:292
  49.7 18.2 %collective-permute-done.5.refs_9_ = bf16[8,64,256]{2,1,0:T(8,128)(2,1)S(1)} collective-permute-done((bf16[8,64,256]{2,1,0:T(8,128)(2,1)S(1)}, bf16[8,64,256]{2,1,0:T(8,128)(2,1)S(1)}, u32[]{:S(2)}, u32[]{:S(2)}) %collective-permute-start.5) | collective-permute-done | bytes 262176 | tf_op jit(solution)/shard_map/ppermute | solution.py:293
  67.8 8.0 %collective-permute-start.7 = (bf16[8,64,256]{2,1,0:T(8,128)(2,1)S(1)}, bf16[8,64,256]{2,1,0:T(8,128)(2,1)S(1)}, u32[]{:S(2)}, u32[]{:S(2)}) collective-permute-start(bf16[8,64,256]{2,1,0:T(8,128)(2,1)S(1)} %collective-permute-done.5.refs_9_), channel_id=1, source_target_pairs={{192,160},{224,192},{256,224},{288,256},{320,288},{352,320},{384,3... | collective-permute-start | bytes 786440 | tf_op jit(solution)/shard_map/ppermute | solution.py:293
  75.8 0.0 copy-start.1
  75.8 0.6 copy-done.1
  76.5 0.0 copy-start.2
  76.5 0.7 copy-done.2
  77.1 2.8 %prepare_queries.1.refs_2_ = bf16[8,128,512]{2,1,0:T(8,128)(2,1)S(1)} custom-call(s32[1]{0:T(128)} %bitcast.where_ref.refs_0_, s32[1,4]{1,0:T(1,128)S(1)} %copy-done.1, bf16[1,64,8192]{2,1,0:T(8,128)(2,1)} %query_hbm.1, f32[1,128]{1,0:T(1,128)S(1)} %bitcast.5), custom_call_target="tpu_custom_call" | custom-call | flops 10000000 | bytes 4194304 | tf_op jit(solution)/shard_map/prepare_queries/pallas_call | solution.py:133
  80.0 0.0 collective-permute-done.8
  80.0 4.6 %attend_early.1 = (f32[8,128,512]{2,1,0:T(8,128)S(1)}, f32[8,8,512]{2,1,0:T(8,128)S(1)}) custom-call(s32[1]{0:T(128)} %bitcast.where_ref.refs_0_, s32[1,4]{1,0:T(1,128)S(1)} %copy-done.1, bf16[8,128,512]{2,1,0:T(8,128)(2,1)S(1)} %prepare_queries.1.refs_2_, bf16[8,64,256]{2,1,0:T(8,128)(2,1)} %prepare_keys.1.refs_3_, ...), custom_call_target="tpu_custom_call" | custom-call | flops 939524096 | bytes 4194304 | tf_op jit(solution)/shard_map/attend_early/pallas_call | solution.py:228
  84.6 0.0 collective-permute-done.6.refs_5_
  84.6 0.0 collective-permute-done.7.refs_6_
  84.6 3.6 %attend_late.1 = bf16[1,64,8192]{2,1,0:T(8,128)(2,1)} custom-call(s32[1]{0:T(128)} %bitcast.where_ref.refs_0_, s32[1,4]{1,0:T(1,128)S(1)} %copy-done.1, bf16[8,128,512]{2,1,0:T(8,128)(2,1)S(1)} %prepare_queries.1.refs_2_, f32[8,128,512]{2,1,0:T(8,128)S(1)} %get-tuple-element.4.refs_3_, f32[8,8,512]{2,1,0:T(8,128)S(1)} %get-tuple-element.5.refs_4_, ...), custom_call_target="tpu_custom_call" | custom-call | flops 268435456 | bytes 4194304 | tf_op jit(solution)/shard_map/attend_late/pallas_call | solution.py:244
  88.2 0.7 copy.9
Async XLA Ops:
  0.6 0.7 copy-start
  4.0 16.1 %collective-permute-start = (bf16[8,64,256]{2,1,0:T(8,128)(2,1)}, bf16[8,64,256]{2,1,0:T(8,128)(2,1)S(1)}, u32[]{:S(2)}, u32[]{:S(2)}) collective-permute-start(bf16[8,64,256]{2,1,0:T(8,128)(2,1)} %prepare_keys.1.refs_3_), channel_id=1, source_target_pairs={{0,32},{32,64},{64,96},{96,128},{128,160},{160,192},{192,224},{224... | collective-permute-start | bytes 786440 | tf_op jit(solution)/shard_map/ppermute | solution.py:289
  7.5 16.1 %collective-permute-start.3 = (bf16[8,64,256]{2,1,0:T(8,128)(2,1)}, bf16[8,64,256]{2,1,0:T(8,128)(2,1)S(1)}, u32[]{:S(2)}, u32[]{:S(2)}) collective-permute-start(bf16[8,64,256]{2,1,0:T(8,128)(2,1)} %prepare_keys.1.refs_3_), channel_id=1, source_target_pairs={{0,256},{32,288},{64,320},{96,352},{128,384},{160,416},{192,448},{... | collective-permute-start | bytes 786440 | tf_op jit(solution)/shard_map/ppermute | solution.py:290
  10.9 33.4 %all-to-all-start = ((bf16[32,16,256]{2,1,0:T(8,128)(2,1)}), bf16[32,16,256]{2,1,0:T(8,128)(2,1)S(1)}, u32[]{:S(2)}, u32[]{:S(2)}) async-start(bf16[32,16,256]{2,1,0:T(8,128)(2,1)} %bitcast.3), calls=%async_computation | async-start | bytes 524288 | tf_op jit(solution)/shard_map/all_to_all | solution.py:296
  20.1 14.7 %collective-permute-start.1 = (bf16[8,64,256]{2,1,0:T(8,128)(2,1)S(1)}, bf16[8,64,256]{2,1,0:T(8,128)(2,1)S(1)}, u32[]{:S(2)}, u32[]{:S(2)}) collective-permute-start(bf16[8,64,256]{2,1,0:T(8,128)(2,1)S(1)} %collective-permute-done.refs_4_), channel_id=1, source_target_pairs={{32,64},{64,96},{96,128},{128,160},{160,192},{192,224},{224,256},{... | collective-permute-start | bytes 786440 | tf_op jit(solution)/shard_map/ppermute | solution.py:292
  23.6 13.1 %collective-permute-start.4 = (bf16[8,64,256]{2,1,0:T(8,128)(2,1)S(1)}, bf16[8,64,256]{2,1,0:T(8,128)(2,1)S(1)}, u32[]{:S(2)}, u32[]{:S(2)}) collective-permute-start(bf16[8,64,256]{2,1,0:T(8,128)(2,1)S(1)} %collective-permute-done.3.refs_7_), channel_id=1, source_target_pairs={{256,224},{288,256},{320,288},{352,320},{384,352},{416,384},{448,4... | collective-permute-start | bytes 786440 | tf_op jit(solution)/shard_map/ppermute | solution.py:293
  34.8 13.0 %collective-permute-start.2 = (bf16[8,64,256]{2,1,0:T(8,128)(2,1)S(1)}, bf16[8,64,256]{2,1,0:T(8,128)(2,1)S(1)}, u32[]{:S(2)}, u32[]{:S(2)}) collective-permute-start(bf16[8,64,256]{2,1,0:T(8,128)(2,1)S(1)} %collective-permute-done.1.refs_5_), channel_id=1, source_target_pairs={{64,96},{96,128},{128,160},{160,192},{192,224},{224,256},{256,288}... | collective-permute-start | bytes 786440 | tf_op jit(solution)/shard_map/ppermute | solution.py:292
  36.7 31.1 %collective-permute-start.5 = (bf16[8,64,256]{2,1,0:T(8,128)(2,1)S(1)}, bf16[8,64,256]{2,1,0:T(8,128)(2,1)S(1)}, u32[]{:S(2)}, u32[]{:S(2)}) collective-permute-start(bf16[8,64,256]{2,1,0:T(8,128)(2,1)S(1)} %collective-permute-done.4.refs_8_), channel_id=1, source_target_pairs={{224,192},{256,224},{288,256},{320,288},{352,320},{384,352},{416,3... | collective-permute-start | bytes 786440 | tf_op jit(solution)/shard_map/ppermute | solution.py:293
  44.2 35.7 %collective-permute-start.8 = (bf16[32,16,256]{2,1,0:T(8,128)(2,1)S(1)}, bf16[32,16,256]{2,1,0:T(8,128)(2,1)S(1)}, u32[]{:S(2)}, u32[]{:S(2)}) collective-permute-start(bf16[32,16,256]{2,1,0:T(8,128)(2,1)S(1)} %all-to-all-done), channel_id=1, source_target_pairs={{0,0},{1,1},{2,2},{3,3},{4,64},{5,65},{6,66},{7,67},{8,128},{9,129... | collective-permute-start | bytes 786440 | tf_op jit(solution)/shard_map/ppermute | solution.py:297
  47.7 36.9 %collective-permute-start.6 = (bf16[8,64,256]{2,1,0:T(8,128)(2,1)S(1)}, bf16[8,64,256]{2,1,0:T(8,128)(2,1)S(1)}, u32[]{:S(2)}, u32[]{:S(2)}) collective-permute-start(bf16[8,64,256]{2,1,0:T(8,128)(2,1)S(1)} %collective-permute-done.2.refs_6_), channel_id=1, source_target_pairs={{96,128},{128,160},{160,192},{192,224},{224,256},{256,288},{288,32... | collective-permute-start | bytes 786440 | tf_op jit(solution)/shard_map/ppermute | solution.py:292
  67.8 16.8 %collective-permute-start.7 = (bf16[8,64,256]{2,1,0:T(8,128)(2,1)S(1)}, bf16[8,64,256]{2,1,0:T(8,128)(2,1)S(1)}, u32[]{:S(2)}, u32[]{:S(2)}) collective-permute-start(bf16[8,64,256]{2,1,0:T(8,128)(2,1)S(1)} %collective-permute-done.5.refs_9_), channel_id=1, source_target_pairs={{192,160},{224,192},{256,224},{288,256},{320,288},{352,320},{384,3... | collective-permute-start | bytes 786440 | tf_op jit(solution)/shard_map/ppermute | solution.py:293
  75.8 0.7 copy-start.1
  76.5 0.7 copy-start.2

commit v2 on v1

--- a/solution.py
+++ b/solution.py
@@ -17,7 +17,7 @@
 ROWS = 64
 REACH = 8
 LOG2E = 1.4426950408889634
-VMEM_LIMIT = 40 * 1024 * 1024
+VMEM_LIMIT = 20 * 1024 * 1024
 
 
 def doc_starts(lens_ref, token):
@@ -92,7 +92,7 @@
         ],
         compiler_params=PARAMS,
         name="prepare_keys",
-    )(where, lens, stay(key), stay(value), stay(gain))
+    )(where, stay(lens), stay(key), stay(value), stay(gain))
 
 
 def query_kernel(where_ref, lens_ref, query_hbm, gain_ref, out_ref, query_ref, sems):
@@ -142,7 +142,7 @@
         compiler_params=PARAMS,
         cost_estimate=pl.CostEstimate(flops=10_000_000, bytes_accessed=4 << 20, transcendentals=0),
         name="prepare_queries",
-    )(where, lens, stay(query), gain)
+    )(where, stay(lens), stay(query), stay(gain))
 
 
 def visible_bias(where_ref, lens_ref, offsets):
@@ -199,8 +199,8 @@
         keep = jnp.exp2(old_top - top)
         weights = jnp.exp2(scores - top)
         denom = stat_ref[h, 1:2, :] * keep + jnp.sum(weights, axis=0, keepdims=True)
-        mixed = (acc_ref[h] * keep + mix_values(h, blocks, weights)) / denom
-        rounded = mixed.astype(jnp.bfloat16)
+        mixed = acc_ref[h] * keep + mix_values(h, blocks, weights)
+        rounded = (mixed * (1.0 / denom)).astype(jnp.bfloat16)
         for c in range(SHARE // 2):
             both = rounded[:, c * 2 * ROWS : (c + 1) * 2 * ROWS].T
             column = (h * SHARE + 2 * c) * HD
@@ -236,7 +236,7 @@
         compiler_params=PARAMS,
         cost_estimate=attention_cost(count),
         name="attend_early",
-    )(where, lens, query, *blocks)
+    )(where, stay(lens), query, *blocks)
 
 
 def attend_late(offsets, where, lens, query, acc, stat, blocks):
@@ -253,7 +253,24 @@
         compiler_params=PARAMS,
         cost_estimate=attention_cost(count),
         name="attend_late",
-    )(where, lens, query, acc, stat, *blocks)
+    )(where, stay(lens), query, acc, stat, *blocks)
+
+
+def pages_kernel(where_ref, kv_ref, out_ref):
+    place = jnp.bitwise_and(where_ref[0], KVH - 1)
+    for h in range(KVH):
+        out_ref[h] = kv_ref[jnp.bitwise_xor(place, h)]
+
+
+def order_pages(where, kv):
+    return pl.pallas_call(
+        pages_kernel,
+        out_shape=jax.ShapeDtypeStruct((KVH, ROWS, 2 * HD), jnp.bfloat16),
+        in_specs=[SMEM_SPEC, VMEM_SPEC],
+        out_specs=VMEM_SPEC,
+        compiler_params=PARAMS,
+        name="order_pages",
+    )(where, kv)
 
 
 def plus_pairs(count, step):
@@ -275,8 +292,8 @@
     for s in range(seqs):
         repeat, place = divmod(s, KVH)
         for g in range(groups):
-            head, page = divmod(g, spread)
-            entry = head * 2 + repeat
+            slot, page = divmod(g, spread)
+            entry = (slot ^ place) * 2 + repeat
             pairs.append((s * groups + g, entry * groups + place * spread + page))
     return pairs
 
@@ -286,31 +303,34 @@
     groups = lax.axis_size("group")
     where = lax.axis_index("seq").astype(jnp.int32).reshape(1)
     kv = prepare_keys(where, doc_lengths, key_proj, value_proj, key_gain.reshape(1, HD))
-    plus = [lax.ppermute(kv, "seq", plus_pairs(seqs, 1))]
-    minus = [lax.ppermute(kv, "seq", cross_pairs(seqs))]
-    for step in (2, 3, 4):
-        plus.append(lax.ppermute(plus[-1], "seq", plus_pairs(seqs, step)))
-        minus.append(lax.ppermute(minus[-1], "seq", minus_pairs(seqs, step - 1)))
-    query = prepare_queries(where, doc_lengths, query_proj, query_gain.reshape(1, HD))
-    pages = kv.reshape(KVH * (ROWS // PAGE), PAGE, 2 * HD)
+    minus8 = lax.ppermute(kv, "seq", cross_pairs(seqs))
+    minus1 = lax.ppermute(kv, "seq", plus_pairs(seqs, 1))
+    pages = order_pages(where, kv).reshape(groups, PAGE, 2 * HD)
     mine = lax.all_to_all(pages, "group", split_axis=0, concat_axis=0, tiled=True)
+    minus8, minus1, later = lax.optimization_barrier((minus8, minus1, where))
+    minus7 = lax.ppermute(minus8, "seq", minus_pairs(seqs, 1))
+    minus2 = lax.ppermute(minus1, "seq", plus_pairs(seqs, 2))
+    query = prepare_queries(later, doc_lengths, query_proj, query_gain.reshape(1, HD))
+    minus7, minus2, query, mine = lax.optimization_barrier((minus7, minus2, query, mine))
+    minus6 = lax.ppermute(minus7, "seq", minus_pairs(seqs, 2))
+    minus3 = lax.ppermute(minus2, "seq", plus_pairs(seqs, 3))
     cache = lax.ppermute(mine, ("seq", "group"), slot_pairs(seqs, groups))
+    minus6, minus3 = lax.optimization_barrier((minus6, minus3))
+    minus5 = lax.ppermute(minus6, "seq", minus_pairs(seqs, 3))
+    minus4 = lax.ppermute(minus3, "seq", plus_pairs(seqs, 4))
     acc, stat = attend_early(
-        (0, 1, 2, 3, 8, 7, 6), where, doc_lengths, query, [kv] + plus[:3] + minus[:3]
+        (0, 1, 8, 2, 7, 3, 6),
+        where,
+        doc_lengths,
+        query,
+        [kv, minus1, minus8, minus2, minus7, minus3, minus6],
     )
-    attended = attend_late((4, 5), where, doc_lengths, query, acc, stat, [plus[3], minus[3]])
+    attended = attend_late((4, 5), where, doc_lengths, query, acc, stat, [minus4, minus5])
     return attended, cache.reshape(1, 1, groups, 1, PAGE, 2 * HD)
 
 
 def solution(mesh):
-    in_specs = (
-        P("group", "seq", None),
-        P("group", "seq", None),
-        P("group", "seq", None),
-        P(),
-        P(),
-        P("group", None),
-    )
-    out_specs = (P("seq", "group", None, None, None, None),)
-    out_specs = (P("group", "seq", None),) + out_specs
+    rows = P("group", "seq", None)
+    in_specs = (rows, rows, rows, P(), P(), P("group", None))
+    out_specs = (rows, P("seq", "group", None, None, None, None))
     return jax.shard_map(body, mesh=mesh, in_specs=in_specs, out_specs=out_specs, check_vma=False)

time: 89.4 us -> 82.6 us (0.924)
  the two profiles are of different devices: /device:TPU:198 before, /device:TPU:250 now
where the time goes in v2:
time: 82.6 us; the launch traced here: 82.2 us
  starting transfers between devices  52.6 us (64%)
  waiting for transfers between devices  14.2 us (17%)
  Pallas kernels  13.9 us (17%)
    ppermute x1, starting transfers between devices, body(): minus4 = lax.ppermute(minus3, 'seq', plus_pairs(seqs, 4))  9.45 us
    all_to_all x1, starting transfers between devices, body(): lax.all_to_all(pages, 'group', split_axis=0, concat_axis=0, tiled=True)  9.21 us
    ppermute x1, starting transfers between devices, body(): minus2 = lax.ppermute(minus1, 'seq', plus_pairs(seqs, 2))  8.16 us
    ppermute x1, starting transfers between devices, body(): minus3 = lax.ppermute(minus2, 'seq', plus_pairs(seqs, 3))  8 us
    ppermute x1, starting transfers between devices, body(): cache = lax.ppermute(mine, ('seq', 'group'), slot_pairs(seqs, groups))  6.11 us
    ppermute x1, waiting for transfers between devices, body(): minus3 = lax.ppermute(minus2, 'seq', plus_pairs(seqs, 3))  5.95 us
    ppermute x1, waiting for transfers between devices, body(): cache = lax.ppermute(mine, ('seq', 'group'), slot_pairs(seqs, groups))  4.91 us
    pallas_call x1, Pallas kernels, attend_early(): pl.pallas_call(lambda *refs: early_kernel(offsets, *refs), out_shape=(jax...  4.32 us
  transfers between devices with their start and end apart: 10, of which 5 were waited for; matrix products, arithmetic and copies ran while one was open for 0% of the time, Pallas kernels for 10%

profile of v2, /device:TPU:250, one launch (start us, length us, event | category | flops | bytes accessed | tf_op | source)
XLA Modules:
  0.0 82.2 jit_solution(18415814047597018092)
XLA Ops:
  0.6 2.2 %prepare_keys.1.kv_ref.refs_3_ = bf16[8,64,256]{2,1,0:T(8,128)(2,1)S(1)} custom-call(s32[1]{0:T(128)} %bitcast.where_ref.refs_0_, s32[1,4]{1,0:T(1,128)} %refs_1_.3, bf16[1,64,1024]{2,1,0:T(8,128)(2,1)} %key_hbm.1, bf16[1,64,1024]{2,1,0:T(8,128)(2,1)} %value_hbm.1, f32[1,128]{1,0:T(1,128)} %bitcast.6), custom_call_target="tpu_custom_call" | custom-call | tf_op jit(solution)/shard_map/prepare_keys/pallas_call | solution.py:82
  2.8 4.0 %collective-permute-start = (bf16[8,64,256]{2,1,0:T(8,128)(2,1)S(1)}, bf16[8,64,256]{2,1,0:T(8,128)(2,1)S(1)}, u32[]{:S(2)}, u32[]{:S(2)}) collective-permute-start(bf16[8,64,256]{2,1,0:T(8,128)(2,1)S(1)} %prepare_keys.1.kv_ref.refs_3_), channel_id=1, source_target_pairs={{0,256},{32,288},{64,320},{96,352},{128,384},{160,416},{192,448},{... | collective-permute-start | bytes 786440 | tf_op jit(solution)/shard_map/ppermute | solution.py:306
  6.9 2.5 %collective-permute-start.1 = (bf16[8,64,256]{2,1,0:T(8,128)(2,1)S(1)}, bf16[8,64,256]{2,1,0:T(8,128)(2,1)S(1)}, u32[]{:S(2)}, u32[]{:S(2)}) collective-permute-start(bf16[8,64,256]{2,1,0:T(8,128)(2,1)S(1)} %prepare_keys.1.kv_ref.refs_3_), channel_id=1, source_target_pairs={{0,32},{32,64},{64,96},{96,128},{128,160},{160,192},{192,224},{224... | collective-permute-start | bytes 786440 | tf_op jit(solution)/shard_map/ppermute | solution.py:307
  9.4 0.7 order_pages.1
  10.1 9.2 %all-to-all-start = ((bf16[32,16,256]{2,1,0:T(8,128)(2,1)}), bf16[32,16,256]{2,1,0:T(8,128)(2,1)S(1)}, u32[]{:S(2)}, u32[]{:S(2)}) async-start(bf16[32,16,256]{2,1,0:T(8,128)(2,1)} %bitcast.3), calls=%async_computation | async-start | bytes 524288 | tf_op jit(solution)/shard_map/all_to_all | solution.py:309
  19.3 0.0 collective-permute-done.refs_5_
  19.3 0.0 collective-permute-done.1.refs_4_
  19.3 1.3 %collective-permute-start.2 = (bf16[8,64,256]{2,1,0:T(8,128)(2,1)S(1)}, bf16[8,64,256]{2,1,0:T(8,128)(2,1)S(1)}, u32[]{:S(2)}, u32[]{:S(2)}) collective-permute-start(bf16[8,64,256]{2,1,0:T(8,128)(2,1)S(1)} %collective-permute-done.refs_5_), channel_id=1, source_target_pairs={{256,224},{288,256},{320,288},{352,320},{384,352},{416,384},{448,4... | collective-permute-start | bytes 786440 | tf_op jit(solution)/shard_map/ppermute | solution.py:311
  20.6 8.2 %collective-permute-start.3 = (bf16[8,64,256]{2,1,0:T(8,128)(2,1)S(1)}, bf16[8,64,256]{2,1,0:T(8,128)(2,1)S(1)}, u32[]{:S(2)}, u32[]{:S(2)}) collective-permute-start(bf16[8,64,256]{2,1,0:T(8,128)(2,1)S(1)} %collective-permute-done.1.refs_4_), channel_id=1, source_target_pairs={{32,64},{64,96},{96,128},{128,160},{160,192},{192,224},{224,256},{... | collective-permute-start | bytes 786440 | tf_op jit(solution)/shard_map/ppermute | solution.py:312
  28.8 2.9 %prepare_queries.1.refs_2_ = bf16[8,128,512]{2,1,0:T(8,128)(2,1)S(1)} custom-call(s32[1]{0:T(128)} %bitcast.where_ref.refs_0_, s32[1,4]{1,0:T(1,128)} %refs_1_.3, bf16[1,64,8192]{2,1,0:T(8,128)(2,1)} %query_hbm.1, f32[1,128]{1,0:T(1,128)} %bitcast.7), custom_call_target="tpu_custom_call" | custom-call | flops 10000000 | bytes 4194304 | tf_op jit(solution)/shard_map/prepare_queries/pallas_call | solution.py:133
  31.8 0.0 all-to-all-done
  31.8 1.4 %collective-permute-done.2.refs_7_ = bf16[8,64,256]{2,1,0:T(8,128)(2,1)S(1)} collective-permute-done((bf16[8,64,256]{2,1,0:T(8,128)(2,1)S(1)}, bf16[8,64,256]{2,1,0:T(8,128)(2,1)S(1)}, u32[]{:S(2)}, u32[]{:S(2)}) %collective-permute-start.2) | collective-permute-done | bytes 262176 | tf_op jit(solution)/shard_map/ppermute | solution.py:311
  33.2 1.2 %collective-permute-done.3.refs_6_ = bf16[8,64,256]{2,1,0:T(8,128)(2,1)S(1)} collective-permute-done((bf16[8,64,256]{2,1,0:T(8,128)(2,1)S(1)}, bf16[8,64,256]{2,1,0:T(8,128)(2,1)S(1)}, u32[]{:S(2)}, u32[]{:S(2)}) %collective-permute-start.3) | collective-permute-done | bytes 262176 | tf_op jit(solution)/shard_map/ppermute | solution.py:312
  34.4 1.9 %collective-permute-start.4 = (bf16[8,64,256]{2,1,0:T(8,128)(2,1)S(1)}, bf16[8,64,256]{2,1,0:T(8,128)(2,1)S(1)}, u32[]{:S(2)}, u32[]{:S(2)}) collective-permute-start(bf16[8,64,256]{2,1,0:T(8,128)(2,1)S(1)} %collective-permute-done.2.refs_7_), channel_id=1, source_target_pairs={{224,192},{256,224},{288,256},{320,288},{352,320},{384,352},{416,3... | collective-permute-start | bytes 786440 | tf_op jit(solution)/shard_map/ppermute | solution.py:315
  36.3 8.0 %collective-permute-start.5 = (bf16[8,64,256]{2,1,0:T(8,128)(2,1)S(1)}, bf16[8,64,256]{2,1,0:T(8,128)(2,1)S(1)}, u32[]{:S(2)}, u32[]{:S(2)}) collective-permute-start(bf16[8,64,256]{2,1,0:T(8,128)(2,1)S(1)} %collective-permute-done.3.refs_6_), channel_id=1, source_target_pairs={{64,96},{96,128},{128,160},{160,192},{192,224},{224,256},{256,288}... | collective-permute-start | bytes 786440 | tf_op jit(solution)/shard_map/ppermute | solution.py:316
  44.3 6.1 %collective-permute-start.8 = (bf16[32,16,256]{2,1,0:T(8,128)(2,1)S(1)}, bf16[32,16,256]{2,1,0:T(8,128)(2,1)S(1)}, u32[]{:S(2)}, u32[]{:S(2)}) collective-permute-start(bf16[32,16,256]{2,1,0:T(8,128)(2,1)S(1)} %all-to-all-done), channel_id=1, source_target_pairs={{0,0},{1,1},{2,2},{3,3},{4,64},{5,65},{6,66},{7,67},{8,128},{9,129... | collective-permute-start | bytes 786440 | tf_op jit(solution)/shard_map/ppermute | solution.py:317
  50.4 0.0 collective-permute-done.4.refs_9_
  50.4 6.0 %collective-permute-done.5.refs_8_ = bf16[8,64,256]{2,1,0:T(8,128)(2,1)S(1)} collective-permute-done((bf16[8,64,256]{2,1,0:T(8,128)(2,1)S(1)}, bf16[8,64,256]{2,1,0:T(8,128)(2,1)S(1)}, u32[]{:S(2)}, u32[]{:S(2)}) %collective-permute-start.5) | collective-permute-done | bytes 262176 | tf_op jit(solution)/shard_map/ppermute | solution.py:316
  56.4 9.5 %collective-permute-start.6 = (bf16[8,64,256]{2,1,0:T(8,128)(2,1)S(1)}, bf16[8,64,256]{2,1,0:T(8,128)(2,1)S(1)}, u32[]{:S(2)}, u32[]{:S(2)}) collective-permute-start(bf16[8,64,256]{2,1,0:T(8,128)(2,1)S(1)} %collective-permute-done.5.refs_8_), channel_id=1, source_target_pairs={{96,128},{128,160},{160,192},{192,224},{224,256},{256,288},{288,32... | collective-permute-start | bytes 786440 | tf_op jit(solution)/shard_map/ppermute | solution.py:320
  65.9 1.9 %collective-permute-start.7 = (bf16[8,64,256]{2,1,0:T(8,128)(2,1)S(1)}, bf16[8,64,256]{2,1,0:T(8,128)(2,1)S(1)}, u32[]{:S(2)}, u32[]{:S(2)}) collective-permute-start(bf16[8,64,256]{2,1,0:T(8,128)(2,1)S(1)} %collective-permute-done.4.refs_9_), channel_id=1, source_target_pairs={{192,160},{224,192},{256,224},{288,256},{320,288},{352,320},{384,3... | collective-permute-start | bytes 786440 | tf_op jit(solution)/shard_map/ppermute | solution.py:319
  67.8 4.9 %collective-permute-done.8 = bf16[32,16,256]{2,1,0:T(8,128)(2,1)S(1)} collective-permute-done((bf16[32,16,256]{2,1,0:T(8,128)(2,1)S(1)}, bf16[32,16,256]{2,1,0:T(8,128)(2,1)S(1)}, u32[]{:S(2)}, u32[]{:S(2)}) %collective-permute-start.8) | collective-permute-done | bytes 262176 | tf_op jit(solution)/shard_map/ppermute | solution.py:317
  72.7 4.3 %attend_early.1 = (f32[8,128,512]{2,1,0:T(8,128)S(1)}, f32[8,8,512]{2,1,0:T(8,128)S(1)}) custom-call(s32[1]{0:T(128)} %bitcast.where_ref.refs_0_, s32[1,4]{1,0:T(1,128)} %refs_1_.3, bf16[8,128,512]{2,1,0:T(8,128)(2,1)S(1)} %prepare_queries.1.refs_2_, bf16[8,64,256]{2,1,0:T(8,128)(2,1)S(1)} %prepare_keys.1.kv_ref.refs_3_, ...), custom_call_target="tpu_custom_call" | custom-call | flops 939524096 | bytes 4194304 | tf_op jit(solution)/shard_map/attend_early/pallas_call | solution.py:228
  77.0 0.0 collective-permute-done.6.refs_5_
  77.0 0.7 collective-permute-done.7.refs_6_
  77.7 3.7 %attend_late.1 = bf16[1,64,8192]{2,1,0:T(8,128)(2,1)} custom-call(s32[1]{0:T(128)} %bitcast.where_ref.refs_0_, s32[1,4]{1,0:T(1,128)} %refs_1_.3, bf16[8,128,512]{2,1,0:T(8,128)(2,1)S(1)} %prepare_queries.1.refs_2_, f32[8,128,512]{2,1,0:T(8,128)S(1)} %get-tuple-element.21.refs_3_, f32[8,8,512]{2,1,0:T(8,128)S(1)} %get-tuple-element.22.refs_4_, ...), custom_call_target="tpu_custom_call" | custom-call | flops 268435456 | bytes 4194304 | tf_op jit(solution)/shard_map/attend_late/pallas_call | solution.py:244
  81.5 0.7 copy.9
Async XLA Ops:
  2.8 16.5 %collective-permute-start = (bf16[8,64,256]{2,1,0:T(8,128)(2,1)S(1)}, bf16[8,64,256]{2,1,0:T(8,128)(2,1)S(1)}, u32[]{:S(2)}, u32[]{:S(2)}) collective-permute-start(bf16[8,64,256]{2,1,0:T(8,128)(2,1)S(1)} %prepare_keys.1.kv_ref.refs_3_), channel_id=1, source_target_pairs={{0,256},{32,288},{64,320},{96,352},{128,384},{160,416},{192,448},{... | collective-permute-start | bytes 786440 | tf_op jit(solution)/shard_map/ppermute | solution.py:306
  6.9 12.5 %collective-permute-start.1 = (bf16[8,64,256]{2,1,0:T(8,128)(2,1)S(1)}, bf16[8,64,256]{2,1,0:T(8,128)(2,1)S(1)}, u32[]{:S(2)}, u32[]{:S(2)}) collective-permute-start(bf16[8,64,256]{2,1,0:T(8,128)(2,1)S(1)} %prepare_keys.1.kv_ref.refs_3_), channel_id=1, source_target_pairs={{0,32},{32,64},{64,96},{96,128},{128,160},{160,192},{192,224},{224... | collective-permute-start | bytes 786440 | tf_op jit(solution)/shard_map/ppermute | solution.py:307
  10.1 21.7 %all-to-all-start = ((bf16[32,16,256]{2,1,0:T(8,128)(2,1)}), bf16[32,16,256]{2,1,0:T(8,128)(2,1)S(1)}, u32[]{:S(2)}, u32[]{:S(2)}) async-start(bf16[32,16,256]{2,1,0:T(8,128)(2,1)} %bitcast.3), calls=%async_computation | async-start | bytes 524288 | tf_op jit(solution)/shard_map/all_to_all | solution.py:309
  19.3 13.9 %collective-permute-start.2 = (bf16[8,64,256]{2,1,0:T(8,128)(2,1)S(1)}, bf16[8,64,256]{2,1,0:T(8,128)(2,1)S(1)}, u32[]{:S(2)}, u32[]{:S(2)}) collective-permute-start(bf16[8,64,256]{2,1,0:T(8,128)(2,1)S(1)} %collective-permute-done.refs_5_), channel_id=1, source_target_pairs={{256,224},{288,256},{320,288},{352,320},{384,352},{416,384},{448,4... | collective-permute-start | bytes 786440 | tf_op jit(solution)/shard_map/ppermute | solution.py:311
  20.6 13.7 %collective-permute-start.3 = (bf16[8,64,256]{2,1,0:T(8,128)(2,1)S(1)}, bf16[8,64,256]{2,1,0:T(8,128)(2,1)S(1)}, u32[]{:S(2)}, u32[]{:S(2)}) collective-permute-start(bf16[8,64,256]{2,1,0:T(8,128)(2,1)S(1)} %collective-permute-done.1.refs_4_), channel_id=1, source_target_pairs={{32,64},{64,96},{96,128},{128,160},{160,192},{192,224},{224,256},{... | collective-permute-start | bytes 786440 | tf_op jit(solution)/shard_map/ppermute | solution.py:312
  34.4 16.1 %collective-permute-start.4 = (bf16[8,64,256]{2,1,0:T(8,128)(2,1)S(1)}, bf16[8,64,256]{2,1,0:T(8,128)(2,1)S(1)}, u32[]{:S(2)}, u32[]{:S(2)}) collective-permute-start(bf16[8,64,256]{2,1,0:T(8,128)(2,1)S(1)} %collective-permute-done.2.refs_7_), channel_id=1, source_target_pairs={{224,192},{256,224},{288,256},{320,288},{352,320},{384,352},{416,3... | collective-permute-start | bytes 786440 | tf_op jit(solution)/shard_map/ppermute | solution.py:315
  36.3 20.1 %collective-permute-start.5 = (bf16[8,64,256]{2,1,0:T(8,128)(2,1)S(1)}, bf16[8,64,256]{2,1,0:T(8,128)(2,1)S(1)}, u32[]{:S(2)}, u32[]{:S(2)}) collective-permute-start(bf16[8,64,256]{2,1,0:T(8,128)(2,1)S(1)} %collective-permute-done.3.refs_6_), channel_id=1, source_target_pairs={{64,96},{96,128},{128,160},{160,192},{192,224},{224,256},{256,288}... | collective-permute-start | bytes 786440 | tf_op jit(solution)/shard_map/ppermute | solution.py:316
  44.3 28.4 %collective-permute-start.8 = (bf16[32,16,256]{2,1,0:T(8,128)(2,1)S(1)}, bf16[32,16,256]{2,1,0:T(8,128)(2,1)S(1)}, u32[]{:S(2)}, u32[]{:S(2)}) collective-permute-start(bf16[32,16,256]{2,1,0:T(8,128)(2,1)S(1)} %all-to-all-done), channel_id=1, source_target_pairs={{0,0},{1,1},{2,2},{3,3},{4,64},{5,65},{6,66},{7,67},{8,128},{9,129... | collective-permute-start | bytes 786440 | tf_op jit(solution)/shard_map/ppermute | solution.py:317
  56.4 20.6 %collective-permute-start.6 = (bf16[8,64,256]{2,1,0:T(8,128)(2,1)S(1)}, bf16[8,64,256]{2,1,0:T(8,128)(2,1)S(1)}, u32[]{:S(2)}, u32[]{:S(2)}) collective-permute-start(bf16[8,64,256]{2,1,0:T(8,128)(2,1)S(1)} %collective-permute-done.5.refs_8_), channel_id=1, source_target_pairs={{96,128},{128,160},{160,192},{192,224},{224,256},{256,288},{288,32... | collective-permute-start | bytes 786440 | tf_op jit(solution)/shard_map/ppermute | solution.py:320
  65.9 11.9 %collective-permute-start.7 = (bf16[8,64,256]{2,1,0:T(8,128)(2,1)S(1)}, bf16[8,64,256]{2,1,0:T(8,128)(2,1)S(1)}, u32[]{:S(2)}, u32[]{:S(2)}) collective-permute-start(bf16[8,64,256]{2,1,0:T(8,128)(2,1)S(1)} %collective-permute-done.4.refs_9_), channel_id=1, source_target_pairs={{192,160},{224,192},{256,224},{288,256},{320,288},{352,320},{384,3... | collective-permute-start | bytes 786440 | tf_op jit(solution)/shard_map/ppermute | solution.py:319

commit v3 on v2

--- a/solution.py
+++ b/solution.py
@@ -160,14 +160,14 @@
     return jnp.concatenate(pieces, axis=0)
 
 
-def masked_scores(h, query_ref, blocks, bias):
-    keys = jnp.concatenate([b[h, :, :HD] for b in blocks], axis=0)
+def masked_scores(h, query_ref, parts, bias):
+    keys = jnp.concatenate([p[:, :HD] for p in parts], axis=0)
     scores = jnp.dot(keys, query_ref[h], preferred_element_type=jnp.float32)
     return scores * (LOG2E / math.sqrt(HD)) + jnp.concatenate([bias] * (SHARE // 2), axis=1)
 
 
-def mix_values(h, blocks, weights):
-    values = jnp.concatenate([b[h, :, HD:] for b in blocks], axis=0)
+def mix_values(parts, weights):
+    values = jnp.concatenate([p[:, HD:] for p in parts], axis=0)
     return lax.dot_general(
         values,
         weights.astype(jnp.bfloat16),
@@ -180,26 +180,32 @@
     blocks, (acc_ref, stat_ref) = refs[: len(offsets)], refs[len(offsets) :]
     bias = visible_bias(where_ref, lens_ref, offsets)
     for h in range(KVH):
-        scores = masked_scores(h, query_ref, blocks, bias)
+        parts = [b[h] for b in blocks]
+        scores = masked_scores(h, query_ref, parts, bias)
         top = jnp.max(scores, axis=0, keepdims=True)
         weights = jnp.exp2(scores - top)
         stat_ref[h, 0:1, :] = top
         stat_ref[h, 1:2, :] = jnp.sum(weights, axis=0, keepdims=True)
-        acc_ref[h] = mix_values(h, blocks, weights)
+        acc_ref[h] = mix_values(parts, weights)
 
 
 def late_kernel(offsets, where_ref, lens_ref, query_ref, acc_ref, stat_ref, *refs):
-    blocks, (out_hbm, out_ref, sems) = refs[: len(offsets)], refs[len(offsets) :]
+    count = len(offsets)
+    blocks, other_ref, (out_hbm, out_ref, sems) = refs[:count], refs[count], refs[count + 1 :]
     bias = visible_bias(where_ref, lens_ref, offsets)
+    own = where_ref[0]
+    use_other = jnp.logical_and(own >= REACH, own < REACH + REACH // 2)
     copies = []
     for h in range(KVH):
-        scores = masked_scores(h, query_ref, blocks, bias)
+        last = jnp.where(use_other, other_ref[h], blocks[-1][h])
+        parts = [b[h] for b in blocks[:-1]] + [last]
+        scores = masked_scores(h, query_ref, parts, bias)
         old_top = stat_ref[h, 0:1, :]
         top = jnp.maximum(old_top, jnp.max(scores, axis=0, keepdims=True))
         keep = jnp.exp2(old_top - top)
         weights = jnp.exp2(scores - top)
         denom = stat_ref[h, 1:2, :] * keep + jnp.sum(weights, axis=0, keepdims=True)
-        mixed = acc_ref[h] * keep + mix_values(h, blocks, weights)
+        mixed = acc_ref[h] * keep + mix_values(parts, weights)
         rounded = (mixed * (1.0 / denom)).astype(jnp.bfloat16)
         for c in range(SHARE // 2):
             both = rounded[:, c * 2 * ROWS : (c + 1) * 2 * ROWS].T
@@ -244,7 +250,7 @@
     return pl.pallas_call(
         lambda *refs: late_kernel(offsets, *refs),
         out_shape=jax.ShapeDtypeStruct((1, ROWS, KVH * SHARE * HD), jnp.bfloat16),
-        in_specs=[SMEM_SPEC, SMEM_SPEC] + [VMEM_SPEC] * (3 + count),
+        in_specs=[SMEM_SPEC, SMEM_SPEC] + [VMEM_SPEC] * (3 + count + 1),
         out_specs=HBM_SPEC,
         scratch_shapes=[
             pltpu.VMEM((ROWS, KVH * SHARE * HD), jnp.bfloat16),
@@ -274,14 +280,25 @@
 
 
 def plus_pairs(count, step):
-    return [(i, i + 1) for i in range(count - 1) if i + 1 >= step]
-
-
-def cross_pairs(count):
-    return [(i, i + REACH) for i in range(REACH)] + [(REACH + i, i) for i in range(3)]
+    receivers = range(step, count)
+    if step == REACH // 2:
+        receivers = [r for r in receivers if r % REACH >= step]
+    return [(r - 1, r) for r in receivers]
+
+
+def diagonal_pairs(count):
+    return [(i, i + REACH - 1) for i in range(count - REACH + 1)] + [
+        (REACH + 1 + i, i) for i in range(2)
+    ]
+
+
+def partner_pairs(count):
+    return [(i, i + REACH) for i in range(count - REACH)]
 
 
 def minus_pairs(count, step):
+    if step == REACH // 2:
+        return [(r + 1, r) for r in range(REACH, REACH + step)]
     receivers = list(range(REACH - step, count)) + list(range(0, 3 - step))
     return [((r + 1) % count, r) for r in receivers]
 
@@ -303,29 +320,28 @@
     groups = lax.axis_size("group")
     where = lax.axis_index("seq").astype(jnp.int32).reshape(1)
     kv = prepare_keys(where, doc_lengths, key_proj, value_proj, key_gain.reshape(1, HD))
-    minus8 = lax.ppermute(kv, "seq", cross_pairs(seqs))
     minus1 = lax.ppermute(kv, "seq", plus_pairs(seqs, 1))
+    minus7 = lax.ppermute(kv, "seq", diagonal_pairs(seqs))
+    minus8 = lax.ppermute(kv, "seq", partner_pairs(seqs))
     pages = order_pages(where, kv).reshape(groups, PAGE, 2 * HD)
     mine = lax.all_to_all(pages, "group", split_axis=0, concat_axis=0, tiled=True)
-    minus8, minus1, later = lax.optimization_barrier((minus8, minus1, where))
-    minus7 = lax.ppermute(minus8, "seq", minus_pairs(seqs, 1))
     minus2 = lax.ppermute(minus1, "seq", plus_pairs(seqs, 2))
+    minus6 = lax.ppermute(minus7, "seq", minus_pairs(seqs, 2))
+    minus1, later = lax.optimization_barrier((minus1, where))
     query = prepare_queries(later, doc_lengths, query_proj, query_gain.reshape(1, HD))
-    minus7, minus2, query, mine = lax.optimization_barrier((minus7, minus2, query, mine))
-    minus6 = lax.ppermute(minus7, "seq", minus_pairs(seqs, 2))
+    minus2, query, mine = lax.optimization_barrier((minus2, query, mine))
     minus3 = lax.ppermute(minus2, "seq", plus_pairs(seqs, 3))
+    minus5 = lax.ppermute(minus6, "seq", minus_pairs(seqs, 3))
     cache = lax.ppermute(mine, ("seq", "group"), slot_pairs(seqs, groups))
-    minus6, minus3 = lax.optimization_barrier((minus6, minus3))
-    minus5 = lax.ppermute(minus6, "seq", minus_pairs(seqs, 3))
-    minus4 = lax.ppermute(minus3, "seq", plus_pairs(seqs, 4))
     acc, stat = attend_early(
-        (0, 1, 8, 2, 7, 3, 6),
-        where,
-        doc_lengths,
-        query,
-        [kv, minus1, minus8, minus2, minus7, minus3, minus6],
-    )
-    attended = attend_late((4, 5), where, doc_lengths, query, acc, stat, [minus4, minus5])
+        (0, 1, 7, 8, 2, 6), where, doc_lengths, query, [kv, minus1, minus7, minus8, minus2, minus6]
+    )
+    minus3, acc = lax.optimization_barrier((minus3, acc))
+    plus4 = lax.ppermute(minus3, "seq", plus_pairs(seqs, 4))
+    minus4 = lax.ppermute(minus5, "seq", minus_pairs(seqs, 4))
+    attended = attend_late(
+        (3, 5, 4), where, doc_lengths, query, acc, stat, [minus3, minus5, plus4, minus4]
+    )
     return attended, cache.reshape(1, 1, groups, 1, PAGE, 2 * HD)
 
 

time: 82.6 us -> 76.3 us (0.924)
  the two profiles are of different devices: /device:TPU:250 before, /device:TPU:48 now
where the time goes in v3:
time: 76.3 us; the launch traced here: 75.8 us
  starting transfers between devices  43.8 us (57%)
  waiting for transfers between devices  16.5 us (22%)
  Pallas kernels  14 us (18%)
  between operations  0.8 us (1%)
    all_to_all x1, starting transfers between devices, body(): lax.all_to_all(pages, 'group', split_axis=0, concat_axis=0, tiled=True)  10.7 us
    ppermute x1, waiting for transfers between devices, body(): plus4 = lax.ppermute(minus3, 'seq', plus_pairs(seqs, 4))  10.2 us
    ppermute x1, starting transfers between devices, body(): cache = lax.ppermute(mine, ('seq', 'group'), slot_pairs(seqs, groups))  9.39 us
    ppermute x1, starting transfers between devices, body(): minus7 = lax.ppermute(kv, 'seq', diagonal_pairs(seqs))  5.73 us
    pallas_call x1, Pallas kernels, attend_early(): pl.pallas_call(lambda *refs: early_kernel(offsets, *refs), out_shape=(jax...  4.14 us
    pallas_call x1, Pallas kernels, attend_late(): pl.pallas_call(lambda *refs: late_kernel(offsets, *refs), out_shape=jax.S...  4 us
    ppermute x1, waiting for transfers between devices, body(): cache = lax.ppermute(mine, ('seq', 'group'), slot_pairs(seqs, groups))  3.97 us
    ppermute x1, starting transfers between devices, body(): minus8 = lax.ppermute(kv, 'seq', partner_pairs(seqs))  3.09 us
  transfers between devices with their start and end apart: 11, of which 3 were waited for; matrix products, arithmetic and copies ran while one was open for 0% of the time, Pallas kernels for 10%

profile of v3, /device:TPU:48, one launch (start us, length us, event | category | flops | bytes accessed | tf_op | source)
XLA Modules:
  0.0 75.8 jit_solution(869667842792651414)
XLA Ops:
  0.6 2.2 %prepare_keys.1.kv_ref.refs_3_ = bf16[8,64,256]{2,1,0:T(8,128)(2,1)S(1)} custom-call(s32[1]{0:T(128)} %bitcast.where_ref.refs_0_, s32[1,4]{1,0:T(1,128)} %refs_1_.3, bf16[1,64,1024]{2,1,0:T(8,128)(2,1)} %key_hbm.1, bf16[1,64,1024]{2,1,0:T(8,128)(2,1)} %value_hbm.1, f32[1,128]{1,0:T(1,128)} %bitcast.6), custom_call_target="tpu_custom_call" | custom-call | tf_op jit(solution)/shard_map/prepare_keys/pallas_call | solution.py:82
  2.8 2.6 %collective-permute-start = (bf16[8,64,256]{2,1,0:T(8,128)(2,1)S(1)}, bf16[8,64,256]{2,1,0:T(8,128)(2,1)S(1)}, u32[]{:S(2)}, u32[]{:S(2)}) collective-permute-start(bf16[8,64,256]{2,1,0:T(8,128)(2,1)S(1)} %prepare_keys.1.kv_ref.refs_3_), channel_id=1, source_target_pairs={{0,32},{32,64},{64,96},{96,128},{128,160},{160,192},{192,224},{224... | collective-permute-start | bytes 786440 | tf_op jit(solution)/shard_map/ppermute | solution.py:323
  5.4 5.7 %collective-permute-start.3 = (bf16[8,64,256]{2,1,0:T(8,128)(2,1)S(1)}, bf16[8,64,256]{2,1,0:T(8,128)(2,1)S(1)}, u32[]{:S(2)}, u32[]{:S(2)}) collective-permute-start(bf16[8,64,256]{2,1,0:T(8,128)(2,1)S(1)} %prepare_keys.1.kv_ref.refs_3_), channel_id=1, source_target_pairs={{0,224},{32,256},{64,288},{96,320},{128,352},{160,384},{192,416},{... | collective-permute-start | bytes 786440 | tf_op jit(solution)/shard_map/ppermute | solution.py:324
  11.1 0.7 order_pages.1
  11.9 10.7 %all-to-all-start = ((bf16[32,16,256]{2,1,0:T(8,128)(2,1)}), bf16[32,16,256]{2,1,0:T(8,128)(2,1)S(1)}, u32[]{:S(2)}, u32[]{:S(2)}) async-start(bf16[32,16,256]{2,1,0:T(8,128)(2,1)} %bitcast.3), calls=%async_computation | async-start | bytes 524288 | tf_op jit(solution)/shard_map/all_to_all | solution.py:327
  22.6 0.0 collective-permute-done.refs_4_
  22.6 2.6 %collective-permute-start.1 = (bf16[8,64,256]{2,1,0:T(8,128)(2,1)S(1)}, bf16[8,64,256]{2,1,0:T(8,128)(2,1)S(1)}, u32[]{:S(2)}, u32[]{:S(2)}) collective-permute-start(bf16[8,64,256]{2,1,0:T(8,128)(2,1)S(1)} %collective-permute-done.refs_4_), channel_id=1, source_target_pairs={{32,64},{64,96},{96,128},{128,160},{160,192},{192,224},{224,256},{... | collective-permute-start | bytes 786440 | tf_op jit(solution)/shard_map/ppermute | solution.py:328
  25.2 0.0 collective-permute-done.3.refs_5_
  25.2 1.3 %collective-permute-start.5 = (bf16[8,64,256]{2,1,0:T(8,128)(2,1)S(1)}, bf16[8,64,256]{2,1,0:T(8,128)(2,1)S(1)}, u32[]{:S(2)}, u32[]{:S(2)}) collective-permute-start(bf16[8,64,256]{2,1,0:T(8,128)(2,1)S(1)} %collective-permute-done.3.refs_5_), channel_id=1, source_target_pairs={{224,192},{256,224},{288,256},{320,288},{352,320},{384,352},{416,3... | collective-permute-start | bytes 786440 | tf_op jit(solution)/shard_map/ppermute | solution.py:329
  26.5 3.1 %collective-permute-start.4 = (bf16[8,64,256]{2,1,0:T(8,128)(2,1)S(1)}, bf16[8,64,256]{2,1,0:T(8,128)(2,1)S(1)}, u32[]{:S(2)}, u32[]{:S(2)}) collective-permute-start(bf16[8,64,256]{2,1,0:T(8,128)(2,1)S(1)} %prepare_keys.1.kv_ref.refs_3_), channel_id=1, source_target_pairs={{0,256},{32,288},{64,320},{96,352},{128,384},{160,416},{192,448},{... | collective-permute-start | bytes 786440 | tf_op jit(solution)/shard_map/ppermute | solution.py:325
  29.6 2.9 %prepare_queries.1.refs_2_ = bf16[8,128,512]{2,1,0:T(8,128)(2,1)S(1)} custom-call(s32[1]{0:T(128)} %bitcast.where_ref.refs_0_, s32[1,4]{1,0:T(1,128)} %refs_1_.3, bf16[1,64,8192]{2,1,0:T(8,128)(2,1)} %query_hbm.1, f32[1,128]{1,0:T(1,128)} %bitcast.7), custom_call_target="tpu_custom_call" | custom-call | flops 10000000 | bytes 4194304 | tf_op jit(solution)/shard_map/prepare_queries/pallas_call | solution.py:133
  32.6 2.3 %all-to-all-done = bf16[32,16,256]{2,1,0:T(8,128)(2,1)S(1)} async-done(((bf16[32,16,256]{2,1,0:T(8,128)(2,1)}), bf16[32,16,256]{2,1,0:T(8,128)(2,1)S(1)}, u32[]{:S(2)}, u32[]{:S(2)}) %all-to-all-start) | async-done | bytes 262176 | tf_op jit(solution)/shard_map/all_to_all | solution.py:327
  34.8 0.0 collective-permute-done.1.refs_7_
  34.8 3.0 %collective-permute-start.2 = (bf16[8,64,256]{2,1,0:T(8,128)(2,1)S(1)}, bf16[8,64,256]{2,1,0:T(8,128)(2,1)S(1)}, u32[]{:S(2)}, u32[]{:S(2)}) collective-permute-start(bf16[8,64,256]{2,1,0:T(8,128)(2,1)S(1)} %collective-permute-done.1.refs_7_), channel_id=1, source_target_pairs={{64,96},{96,128},{128,160},{160,192},{192,224},{224,256},{256,288}... | collective-permute-start | bytes 786440 | tf_op jit(solution)/shard_map/ppermute | solution.py:333
  37.8 0.0 collective-permute-done.5.refs_8_
  37.8 2.8 %collective-permute-start.6 = (bf16[8,64,256]{2,1,0:T(8,128)(2,1)S(1)}, bf16[8,64,256]{2,1,0:T(8,128)(2,1)S(1)}, u32[]{:S(2)}, u32[]{:S(2)}) collective-permute-start(bf16[8,64,256]{2,1,0:T(8,128)(2,1)S(1)} %collective-permute-done.5.refs_8_), channel_id=1, source_target_pairs={{192,160},{224,192},{256,224},{288,256},{320,288},{352,320},{384,3... | collective-permute-start | bytes 786440 | tf_op jit(solution)/shard_map/ppermute | solution.py:334
  40.7 9.4 %collective-permute-start.9 = (bf16[32,16,256]{2,1,0:T(8,128)(2,1)S(1)}, bf16[32,16,256]{2,1,0:T(8,128)(2,1)S(1)}, u32[]{:S(2)}, u32[]{:S(2)}) collective-permute-start(bf16[32,16,256]{2,1,0:T(8,128)(2,1)S(1)} %all-to-all-done), channel_id=1, source_target_pairs={{0,0},{1,1},{2,2},{3,3},{4,64},{5,65},{6,66},{7,67},{8,128},{9,129... | collective-permute-start | bytes 786440 | tf_op jit(solution)/shard_map/ppermute | solution.py:335
  50.1 0.0 collective-permute-done.4.refs_6_
  50.1 4.1 %attend_early.1 = (f32[8,128,512]{2,1,0:T(8,128)S(1)}, f32[8,8,512]{2,1,0:T(8,128)S(1)}) custom-call(s32[1]{0:T(128)} %bitcast.where_ref.refs_0_, s32[1,4]{1,0:T(1,128)} %refs_1_.3, bf16[8,128,512]{2,1,0:T(8,128)(2,1)S(1)} %prepare_queries.1.refs_2_, bf16[8,64,256]{2,1,0:T(8,128)(2,1)S(1)} %prepare_keys.1.kv_ref.refs_3_, ...), custom_call_target="tpu_custom_call" | custom-call | flops 805306368 | bytes 4194304 | tf_op jit(solution)/shard_map/attend_early/pallas_call | solution.py:234
  54.2 0.0 collective-permute-done.2.refs_5_
  54.2 1.9 %collective-permute-start.7 = (bf16[8,64,256]{2,1,0:T(8,128)(2,1)S(1)}, bf16[8,64,256]{2,1,0:T(8,128)(2,1)S(1)}, u32[]{:S(2)}, u32[]{:S(2)}) collective-permute-start(bf16[8,64,256]{2,1,0:T(8,128)(2,1)S(1)} %collective-permute-done.2.refs_5_), channel_id=1, source_target_pairs={{96,128},{128,160},{160,192},{192,224},{352,384},{384,416},{416,44... | collective-permute-start | bytes 786440 | tf_op jit(solution)/shard_map/ppermute | solution.py:340
  56.2 0.0 collective-permute-done.6.refs_6_
  56.2 0.7 collective-permute-start.8
  56.9 4.0 %collective-permute-done.9 = bf16[32,16,256]{2,1,0:T(8,128)(2,1)S(1)} collective-permute-done((bf16[32,16,256]{2,1,0:T(8,128)(2,1)S(1)}, bf16[32,16,256]{2,1,0:T(8,128)(2,1)S(1)}, u32[]{:S(2)}, u32[]{:S(2)}) %collective-permute-start.9) | collective-permute-done | bytes 262176 | tf_op jit(solution)/shard_map/ppermute | solution.py:335
  60.8 10.2 %collective-permute-done.7.refs_7_ = bf16[8,64,256]{2,1,0:T(8,128)(2,1)S(1)} collective-permute-done((bf16[8,64,256]{2,1,0:T(8,128)(2,1)S(1)}, bf16[8,64,256]{2,1,0:T(8,128)(2,1)S(1)}, u32[]{:S(2)}, u32[]{:S(2)}) %collective-permute-start.7) | collective-permute-done | bytes 262176 | tf_op jit(solution)/shard_map/ppermute | solution.py:340
  71.1 0.0 collective-permute-done.8.refs_8_
  71.1 4.0 %attend_late.1 = bf16[1,64,8192]{2,1,0:T(8,128)(2,1)} custom-call(s32[1]{0:T(128)} %bitcast.where_ref.refs_0_, s32[1,4]{1,0:T(1,128)} %refs_1_.3, bf16[8,128,512]{2,1,0:T(8,128)(2,1)S(1)} %prepare_queries.1.refs_2_, f32[8,128,512]{2,1,0:T(8,128)S(1)} %get-tuple-element.16.refs_3_, f32[8,8,512]{2,1,0:T(8,128)S(1)} %get-tuple-element.17.refs_4_, ...), custom_call_target="tpu_custom_call" | custom-call | flops 402653184 | bytes 4194304 | tf_op jit(solution)/shard_map/attend_late/pallas_call | solution.py:250
  75.1 0.7 copy.9
Async XLA Ops:
  2.8 19.8 %collective-permute-start = (bf16[8,64,256]{2,1,0:T(8,128)(2,1)S(1)}, bf16[8,64,256]{2,1,0:T(8,128)(2,1)S(1)}, u32[]{:S(2)}, u32[]{:S(2)}) collective-permute-start(bf16[8,64,256]{2,1,0:T(8,128)(2,1)S(1)} %prepare_keys.1.kv_ref.refs_3_), channel_id=1, source_target_pairs={{0,32},{32,64},{64,96},{96,128},{128,160},{160,192},{192,224},{224... | collective-permute-start | bytes 786440 | tf_op jit(solution)/shard_map/ppermute | solution.py:323
  5.4 19.8 %collective-permute-start.3 = (bf16[8,64,256]{2,1,0:T(8,128)(2,1)S(1)}, bf16[8,64,256]{2,1,0:T(8,128)(2,1)S(1)}, u32[]{:S(2)}, u32[]{:S(2)}) collective-permute-start(bf16[8,64,256]{2,1,0:T(8,128)(2,1)S(1)} %prepare_keys.1.kv_ref.refs_3_), channel_id=1, source_target_pairs={{0,224},{32,256},{64,288},{96,320},{128,352},{160,384},{192,416},{... | collective-permute-start | bytes 786440 | tf_op jit(solution)/shard_map/ppermute | solution.py:324
  11.9 23.0 %all-to-all-start = ((bf16[32,16,256]{2,1,0:T(8,128)(2,1)}), bf16[32,16,256]{2,1,0:T(8,128)(2,1)S(1)}, u32[]{:S(2)}, u32[]{:S(2)}) async-start(bf16[32,16,256]{2,1,0:T(8,128)(2,1)} %bitcast.3), calls=%async_computation | async-start | bytes 524288 | tf_op jit(solution)/shard_map/all_to_all | solution.py:327
  22.6 12.2 %collective-permute-start.1 = (bf16[8,64,256]{2,1,0:T(8,128)(2,1)S(1)}, bf16[8,64,256]{2,1,0:T(8,128)(2,1)S(1)}, u32[]{:S(2)}, u32[]{:S(2)}) collective-permute-start(bf16[8,64,256]{2,1,0:T(8,128)(2,1)S(1)} %collective-permute-done.refs_4_), channel_id=1, source_target_pairs={{32,64},{64,96},{96,128},{128,160},{160,192},{192,224},{224,256},{... | collective-permute-start | bytes 786440 | tf_op jit(solution)/shard_map/ppermute | solution.py:328
  25.2 12.6 %collective-permute-start.5 = (bf16[8,64,256]{2,1,0:T(8,128)(2,1)S(1)}, bf16[8,64,256]{2,1,0:T(8,128)(2,1)S(1)}, u32[]{:S(2)}, u32[]{:S(2)}) collective-permute-start(bf16[8,64,256]{2,1,0:T(8,128)(2,1)S(1)} %collective-permute-done.3.refs_5_), channel_id=1, source_target_pairs={{224,192},{256,224},{288,256},{320,288},{352,320},{384,352},{416,3... | collective-permute-start | bytes 786440 | tf_op jit(solution)/shard_map/ppermute | solution.py:329
  26.5 23.6 %collective-permute-start.4 = (bf16[8,64,256]{2,1,0:T(8,128)(2,1)S(1)}, bf16[8,64,256]{2,1,0:T(8,128)(2,1)S(1)}, u32[]{:S(2)}, u32[]{:S(2)}) collective-permute-start(bf16[8,64,256]{2,1,0:T(8,128)(2,1)S(1)} %prepare_keys.1.kv_ref.refs_3_), channel_id=1, source_target_pairs={{0,256},{32,288},{64,320},{96,352},{128,384},{160,416},{192,448},{... | collective-permute-start | bytes 786440 | tf_op jit(solution)/shard_map/ppermute | solution.py:325
  34.8 19.4 %collective-permute-start.2 = (bf16[8,64,256]{2,1,0:T(8,128)(2,1)S(1)}, bf16[8,64,256]{2,1,0:T(8,128)(2,1)S(1)}, u32[]{:S(2)}, u32[]{:S(2)}) collective-permute-start(bf16[8,64,256]{2,1,0:T(8,128)(2,1)S(1)} %collective-permute-done.1.refs_7_), channel_id=1, source_target_pairs={{64,96},{96,128},{128,160},{160,192},{192,224},{224,256},{256,288}... | collective-permute-start | bytes 786440 | tf_op jit(solution)/shard_map/ppermute | solution.py:333
  37.8 18.3 %collective-permute-start.6 = (bf16[8,64,256]{2,1,0:T(8,128)(2,1)S(1)}, bf16[8,64,256]{2,1,0:T(8,128)(2,1)S(1)}, u32[]{:S(2)}, u32[]{:S(2)}) collective-permute-start(bf16[8,64,256]{2,1,0:T(8,128)(2,1)S(1)} %collective-permute-done.5.refs_8_), channel_id=1, source_target_pairs={{192,160},{224,192},{256,224},{288,256},{320,288},{352,320},{384,3... | collective-permute-start | bytes 786440 | tf_op jit(solution)/shard_map/ppermute | solution.py:334
  40.7 20.2 %collective-permute-start.9 = (bf16[32,16,256]{2,1,0:T(8,128)(2,1)S(1)}, bf16[32,16,256]{2,1,0:T(8,128)(2,1)S(1)}, u32[]{:S(2)}, u32[]{:S(2)}) collective-permute-start(bf16[32,16,256]{2,1,0:T(8,128)(2,1)S(1)} %all-to-all-done), channel_id=1, source_target_pairs={{0,0},{1,1},{2,2},{3,3},{4,64},{5,65},{6,66},{7,67},{8,128},{9,129... | collective-permute-start | bytes 786440 | tf_op jit(solution)/shard_map/ppermute | solution.py:335
  54.2 16.8 %collective-permute-start.7 = (bf16[8,64,256]{2,1,0:T(8,128)(2,1)S(1)}, bf16[8,64,256]{2,1,0:T(8,128)(2,1)S(1)}, u32[]{:S(2)}, u32[]{:S(2)}) collective-permute-start(bf16[8,64,256]{2,1,0:T(8,128)(2,1)S(1)} %collective-permute-done.2.refs_5_), channel_id=1, source_target_pairs={{96,128},{128,160},{160,192},{192,224},{352,384},{384,416},{416,44... | collective-permute-start | bytes 786440 | tf_op jit(solution)/shard_map/ppermute | solution.py:340
  56.2 14.9 %collective-permute-start.8 = (bf16[8,64,256]{2,1,0:T(8,128)(2,1)S(1)}, bf16[8,64,256]{2,1,0:T(8,128)(2,1)S(1)}, u32[]{:S(2)}, u32[]{:S(2)}) collective-permute-start(bf16[8,64,256]{2,1,0:T(8,128)(2,1)S(1)} %collective-permute-done.6.refs_6_), channel_id=1, source_target_pairs={{288,256},{320,288},{352,320},{384,352},{289,257},{321,289},{353,3... | collective-permute-start | bytes 786440 | tf_op jit(solution)/shard_map/ppermute | solution.py:341

commit v4 on v3

--- a/solution.py
+++ b/solution.py
@@ -189,9 +189,12 @@
         acc_ref[h] = mix_values(parts, weights)
 
 
-def late_kernel(offsets, where_ref, lens_ref, query_ref, acc_ref, stat_ref, *refs):
+def late_kernel(offsets, where_ref, lens_ref, query_ref, acc_ref, stat_ref, cache_ref, *refs):
     count = len(offsets)
-    blocks, other_ref, (out_hbm, out_ref, sems) = refs[:count], refs[count], refs[count + 1 :]
+    blocks, other_ref = refs[:count], refs[count]
+    out_hbm, cache_hbm, out_ref, sems, cache_sem = refs[count + 1 :]
+    cache_copy = pltpu.make_async_copy(cache_ref, cache_hbm, cache_sem)
+    cache_copy.start()
     bias = visible_bias(where_ref, lens_ref, offsets)
     own = where_ref[0]
     use_other = jnp.logical_and(own >= REACH, own < REACH + REACH // 2)
@@ -219,6 +222,7 @@
         copies[-1].start()
     for copy in copies:
         copy.wait()
+    cache_copy.wait()
 
 
 def attention_cost(count):
@@ -245,21 +249,25 @@
     )(where, stay(lens), query, *blocks)
 
 
-def attend_late(offsets, where, lens, query, acc, stat, blocks):
+def attend_late(offsets, where, lens, query, acc, stat, cache, blocks):
     count = len(offsets)
     return pl.pallas_call(
         lambda *refs: late_kernel(offsets, *refs),
-        out_shape=jax.ShapeDtypeStruct((1, ROWS, KVH * SHARE * HD), jnp.bfloat16),
-        in_specs=[SMEM_SPEC, SMEM_SPEC] + [VMEM_SPEC] * (3 + count + 1),
-        out_specs=HBM_SPEC,
+        out_shape=(
+            jax.ShapeDtypeStruct((1, ROWS, KVH * SHARE * HD), jnp.bfloat16),
+            jax.ShapeDtypeStruct(cache.shape, cache.dtype),
+        ),
+        in_specs=[SMEM_SPEC, SMEM_SPEC] + [VMEM_SPEC] * (4 + count + 1),
+        out_specs=(HBM_SPEC, HBM_SPEC),
         scratch_shapes=[
             pltpu.VMEM((ROWS, KVH * SHARE * HD), jnp.bfloat16),
             pltpu.SemaphoreType.DMA((KVH,)),
+            pltpu.SemaphoreType.DMA(()),
         ],
         compiler_params=PARAMS,
         cost_estimate=attention_cost(count),
         name="attend_late",
-    )(where, stay(lens), query, acc, stat, *blocks)
+    )(where, stay(lens), query, acc, stat, cache, *blocks)
 
 
 def pages_kernel(where_ref, kv_ref, out_ref):
@@ -333,14 +341,17 @@
     minus3 = lax.ppermute(minus2, "seq", plus_pairs(seqs, 3))
     minus5 = lax.ppermute(minus6, "seq", minus_pairs(seqs, 3))
     cache = lax.ppermute(mine, ("seq", "group"), slot_pairs(seqs, groups))
-    acc, stat = attend_early(
-        (0, 1, 7, 8, 2, 6), where, doc_lengths, query, [kv, minus1, minus7, minus8, minus2, minus6]
-    )
-    minus3, acc = lax.optimization_barrier((minus3, acc))
     plus4 = lax.ppermute(minus3, "seq", plus_pairs(seqs, 4))
     minus4 = lax.ppermute(minus5, "seq", minus_pairs(seqs, 4))
-    attended = attend_late(
-        (3, 5, 4), where, doc_lengths, query, acc, stat, [minus3, minus5, plus4, minus4]
+    acc, stat = attend_early(
+        (0, 1, 7, 8, 2, 6, 3, 5),
+        where,
+        doc_lengths,
+        query,
+        [kv, minus1, minus7, minus8, minus2, minus6, minus3, minus5],
+    )
+    attended, cache = attend_late(
+        (4,), where, doc_lengths, query, acc, stat, cache, [plus4, minus4]
     )
     return attended, cache.reshape(1, 1, groups, 1, PAGE, 2 * HD)
 

time: 76.3 us -> 75.7 us (level)
  the two profiles are of different devices: /device:TPU:48 before, /device:TPU:42 now
where the time goes in v4:
time: 75.7 us; the launch traced here: 75.2 us
  starting transfers between devices  39.6 us (52%)
  waiting for transfers between devices  21 us (28%)
  Pallas kernels  13.9 us (18%)
  between operations  0.8 us (1%)
    all_to_all x1, starting transfers between devices, body(): lax.all_to_all(pages, 'group', split_axis=0, concat_axis=0, tiled=True)  11.9 us
    ppermute x1, waiting for transfers between devices, body(): cache = lax.ppermute(mine, ('seq', 'group'), slot_pairs(seqs, groups))  9.63 us
    ppermute x1, starting transfers between devices, body(): cache = lax.ppermute(mine, ('seq', 'group'), slot_pairs(seqs, groups))  6.76 us
    all_to_all x1, waiting for transfers between devices, body(): lax.all_to_all(pages, 'group', split_axis=0, concat_axis=0, tiled=True)  5.83 us
    ppermute x1, waiting for transfers between devices, body(): plus4 = lax.ppermute(minus3, 'seq', plus_pairs(seqs, 4))  5.48 us
    ppermute x1, starting transfers between devices, body(): minus7 = lax.ppermute(kv, 'seq', diagonal_pairs(seqs))  4.83 us
    pallas_call x1, Pallas kernels, attend_early(): pl.pallas_call(lambda *refs: early_kernel(offsets, *refs), out_shape=(jax...  4.59 us
    pallas_call x1, Pallas kernels, attend_late(): pl.pallas_call(lambda *refs: late_kernel(offsets, *refs), out_shape=(jax....  3.46 us
  transfers between devices with their start and end apart: 11, of which 3 were waited for; matrix products, arithmetic and copies ran while one was open for 0% of the time, Pallas kernels for 11%

profile of v4, /device:TPU:42, one launch (start us, length us, event | category | flops | bytes accessed | tf_op | source)
XLA Modules:
  0.0 75.2 jit_solution(12331866184279315454)
XLA Ops:
  0.6 2.2 %prepare_keys.1.kv_ref.refs_3_ = bf16[8,64,256]{2,1,0:T(8,128)(2,1)S(1)} custom-call(s32[1]{0:T(128)} %bitcast.where_ref.refs_0_, s32[1,4]{1,0:T(1,128)} %refs_1_.3, bf16[1,64,1024]{2,1,0:T(8,128)(2,1)} %key_hbm.1, bf16[1,64,1024]{2,1,0:T(8,128)(2,1)} %value_hbm.1, f32[1,128]{1,0:T(1,128)} %bitcast.7), custom_call_target="tpu_custom_call" | custom-call | tf_op jit(solution)/shard_map/prepare_keys/pallas_call | solution.py:82
  2.8 2.6 %collective-permute-start = (bf16[8,64,256]{2,1,0:T(8,128)(2,1)S(1)}, bf16[8,64,256]{2,1,0:T(8,128)(2,1)S(1)}, u32[]{:S(2)}, u32[]{:S(2)}) collective-permute-start(bf16[8,64,256]{2,1,0:T(8,128)(2,1)S(1)} %prepare_keys.1.kv_ref.refs_3_), channel_id=1, source_target_pairs={{0,32},{32,64},{64,96},{96,128},{128,160},{160,192},{192,224},{224... | collective-permute-start | bytes 786440 | tf_op jit(solution)/shard_map/ppermute | solution.py:331
  5.4 4.8 %collective-permute-start.2 = (bf16[8,64,256]{2,1,0:T(8,128)(2,1)S(1)}, bf16[8,64,256]{2,1,0:T(8,128)(2,1)S(1)}, u32[]{:S(2)}, u32[]{:S(2)}) collective-permute-start(bf16[8,64,256]{2,1,0:T(8,128)(2,1)S(1)} %prepare_keys.1.kv_ref.refs_3_), channel_id=1, source_target_pairs={{0,224},{32,256},{64,288},{96,320},{128,352},{160,384},{192,416},{... | collective-permute-start | bytes 786440 | tf_op jit(solution)/shard_map/ppermute | solution.py:332
  10.2 0.7 order_pages.1
  11.0 11.9 %all-to-all-start = ((bf16[32,16,256]{2,1,0:T(8,128)(2,1)}), bf16[32,16,256]{2,1,0:T(8,128)(2,1)S(1)}, u32[]{:S(2)}, u32[]{:S(2)}) async-start(bf16[32,16,256]{2,1,0:T(8,128)(2,1)} %bitcast.3), calls=%async_computation | async-start | bytes 524288 | tf_op jit(solution)/shard_map/all_to_all | solution.py:335
  22.9 0.0 collective-permute-done.refs_4_
  22.9 2.6 %collective-permute-start.1 = (bf16[8,64,256]{2,1,0:T(8,128)(2,1)S(1)}, bf16[8,64,256]{2,1,0:T(8,128)(2,1)S(1)}, u32[]{:S(2)}, u32[]{:S(2)}) collective-permute-start(bf16[8,64,256]{2,1,0:T(8,128)(2,1)S(1)} %collective-permute-done.refs_4_), channel_id=1, source_target_pairs={{32,64},{64,96},{96,128},{128,160},{160,192},{192,224},{224,256},{... | collective-permute-start | bytes 786440 | tf_op jit(solution)/shard_map/ppermute | solution.py:336
  25.5 0.0 collective-permute-done.2.refs_5_
  25.5 0.7 collective-permute-start.4
  26.2 2.9 %prepare_queries.1.refs_2_ = bf16[8,128,512]{2,1,0:T(8,128)(2,1)S(1)} custom-call(s32[1]{0:T(128)} %bitcast.where_ref.refs_0_, s32[1,4]{1,0:T(1,128)} %refs_1_.3, bf16[1,64,8192]{2,1,0:T(8,128)(2,1)} %query_hbm.1, f32[1,128]{1,0:T(1,128)} %bitcast.8), custom_call_target="tpu_custom_call" | custom-call | flops 10000000 | bytes 4194304 | tf_op jit(solution)/shard_map/prepare_queries/pallas_call | solution.py:133
  29.2 5.8 %all-to-all-done = bf16[32,16,256]{2,1,0:T(8,128)(2,1)S(1)} async-done(((bf16[32,16,256]{2,1,0:T(8,128)(2,1)}), bf16[32,16,256]{2,1,0:T(8,128)(2,1)S(1)}, u32[]{:S(2)}, u32[]{:S(2)}) %all-to-all-start) | async-done | bytes 262176 | tf_op jit(solution)/shard_map/all_to_all | solution.py:335
  35.0 0.0 collective-permute-done.1.refs_7_
  35.0 2.6 %collective-permute-start.5 = (bf16[8,64,256]{2,1,0:T(8,128)(2,1)S(1)}, bf16[8,64,256]{2,1,0:T(8,128)(2,1)S(1)}, u32[]{:S(2)}, u32[]{:S(2)}) collective-permute-start(bf16[8,64,256]{2,1,0:T(8,128)(2,1)S(1)} %collective-permute-done.1.refs_7_), channel_id=1, source_target_pairs={{64,96},{96,128},{128,160},{160,192},{192,224},{224,256},{256,288}... | collective-permute-start | bytes 786440 | tf_op jit(solution)/shard_map/ppermute | solution.py:341
  37.6 0.0 collective-permute-done.4.refs_8_
  37.6 1.3 %collective-permute-start.6 = (bf16[8,64,256]{2,1,0:T(8,128)(2,1)S(1)}, bf16[8,64,256]{2,1,0:T(8,128)(2,1)S(1)}, u32[]{:S(2)}, u32[]{:S(2)}) collective-permute-start(bf16[8,64,256]{2,1,0:T(8,128)(2,1)S(1)} %collective-permute-done.4.refs_8_), channel_id=1, source_target_pairs={{192,160},{224,192},{256,224},{288,256},{320,288},{352,320},{384,3... | collective-permute-start | bytes 786440 | tf_op jit(solution)/shard_map/ppermute | solution.py:342
  38.9 2.5 %collective-permute-start.3 = (bf16[8,64,256]{2,1,0:T(8,128)(2,1)S(1)}, bf16[8,64,256]{2,1,0:T(8,128)(2,1)S(1)}, u32[]{:S(2)}, u32[]{:S(2)}) collective-permute-start(bf16[8,64,256]{2,1,0:T(8,128)(2,1)S(1)} %prepare_keys.1.kv_ref.refs_3_), channel_id=1, source_target_pairs={{0,256},{32,288},{64,320},{96,352},{128,384},{160,416},{192,448},{... | collective-permute-start | bytes 786440 | tf_op jit(solution)/shard_map/ppermute | solution.py:333
  41.4 6.8 %collective-permute-start.7 = (bf16[32,16,256]{2,1,0:T(8,128)(2,1)S(1)}, bf16[32,16,256]{2,1,0:T(8,128)(2,1)S(1)}, u32[]{:S(2)}, u32[]{:S(2)}) collective-permute-start(bf16[32,16,256]{2,1,0:T(8,128)(2,1)S(1)} %all-to-all-done), channel_id=1, source_target_pairs={{0,0},{1,1},{2,2},{3,3},{4,64},{5,65},{6,66},{7,67},{8,128},{9,129... | collective-permute-start | bytes 786440 | tf_op jit(solution)/shard_map/ppermute | solution.py:343
  48.1 0.0 collective-permute-done.5.refs_9_
  48.1 3.2 %collective-permute-start.8 = (bf16[8,64,256]{2,1,0:T(8,128)(2,1)S(1)}, bf16[8,64,256]{2,1,0:T(8,128)(2,1)S(1)}, u32[]{:S(2)}, u32[]{:S(2)}) collective-permute-start(bf16[8,64,256]{2,1,0:T(8,128)(2,1)S(1)} %collective-permute-done.5.refs_9_), channel_id=1, source_target_pairs={{96,128},{128,160},{160,192},{192,224},{352,384},{384,416},{416,44... | collective-permute-start | bytes 786440 | tf_op jit(solution)/shard_map/ppermute | solution.py:344
  51.4 0.0 collective-permute-done.6.refs_10_
  51.4 0.7 collective-permute-start.9
  52.0 0.0 collective-permute-done.3.refs_6_
  52.1 4.6 %attend_early.1 = (f32[8,128,512]{2,1,0:T(8,128)S(1)}, f32[8,8,512]{2,1,0:T(8,128)S(1)}) custom-call(s32[1]{0:T(128)} %bitcast.where_ref.refs_0_, s32[1,4]{1,0:T(1,128)} %refs_1_.3, bf16[8,128,512]{2,1,0:T(8,128)(2,1)S(1)} %prepare_queries.1.refs_2_, bf16[8,64,256]{2,1,0:T(8,128)(2,1)S(1)} %prepare_keys.1.kv_ref.refs_3_, ...), custom_call_target="tpu_custom_call" | custom-call | flops 1073741824 | bytes 4194304 | tf_op jit(solution)/shard_map/attend_early/pallas_call | solution.py:238
  56.7 9.6 %collective-permute-done.7.refs_5_ = bf16[32,16,256]{2,1,0:T(8,128)(2,1)S(1)} collective-permute-done((bf16[32,16,256]{2,1,0:T(8,128)(2,1)S(1)}, bf16[32,16,256]{2,1,0:T(8,128)(2,1)S(1)}, u32[]{:S(2)}, u32[]{:S(2)}) %collective-permute-start.7) | collective-permute-done | bytes 262176 | tf_op jit(solution)/shard_map/ppermute | solution.py:343
  66.3 5.5 %collective-permute-done.8.refs_6_ = bf16[8,64,256]{2,1,0:T(8,128)(2,1)S(1)} collective-permute-done((bf16[8,64,256]{2,1,0:T(8,128)(2,1)S(1)}, bf16[8,64,256]{2,1,0:T(8,128)(2,1)S(1)}, u32[]{:S(2)}, u32[]{:S(2)}) %collective-permute-start.8) | collective-permute-done | bytes 262176 | tf_op jit(solution)/shard_map/ppermute | solution.py:344
  71.8 0.0 collective-permute-done.9.refs_7_
  71.8 3.5 %attend_late.1 = (bf16[1,64,8192]{2,1,0:T(8,128)(2,1)}, bf16[32,16,256]{2,1,0:T(8,128)(2,1)}) custom-call(s32[1]{0:T(128)} %bitcast.where_ref.refs_0_, s32[1,4]{1,0:T(1,128)} %refs_1_.3, bf16[8,128,512]{2,1,0:T(8,128)(2,1)S(1)} %prepare_queries.1.refs_2_, f32[8,128,512]{2,1,0:T(8,128)S(1)} %get-tuple-element.15.refs_3_, ...), custom_call_target="tpu_custom_call" | custom-call | flops 134217728 | bytes 4194304 | tf_op jit(solution)/shard_map/attend_late/pallas_call | solution.py:254
Async XLA Ops:
  2.8 20.1 %collective-permute-start = (bf16[8,64,256]{2,1,0:T(8,128)(2,1)S(1)}, bf16[8,64,256]{2,1,0:T(8,128)(2,1)S(1)}, u32[]{:S(2)}, u32[]{:S(2)}) collective-permute-start(bf16[8,64,256]{2,1,0:T(8,128)(2,1)S(1)} %prepare_keys.1.kv_ref.refs_3_), channel_id=1, source_target_pairs={{0,32},{32,64},{64,96},{96,128},{128,160},{160,192},{192,224},{224... | collective-permute-start | bytes 786440 | tf_op jit(solution)/shard_map/ppermute | solution.py:331
  5.4 20.1 %collective-permute-start.2 = (bf16[8,64,256]{2,1,0:T(8,128)(2,1)S(1)}, bf16[8,64,256]{2,1,0:T(8,128)(2,1)S(1)}, u32[]{:S(2)}, u32[]{:S(2)}) collective-permute-start(bf16[8,64,256]{2,1,0:T(8,128)(2,1)S(1)} %prepare_keys.1.kv_ref.refs_3_), channel_id=1, source_target_pairs={{0,224},{32,256},{64,288},{96,320},{128,352},{160,384},{192,416},{... | collective-permute-start | bytes 786440 | tf_op jit(solution)/shard_map/ppermute | solution.py:332
  11.0 24.0 %all-to-all-start = ((bf16[32,16,256]{2,1,0:T(8,128)(2,1)}), bf16[32,16,256]{2,1,0:T(8,128)(2,1)S(1)}, u32[]{:S(2)}, u32[]{:S(2)}) async-start(bf16[32,16,256]{2,1,0:T(8,128)(2,1)} %bitcast.3), calls=%async_computation | async-start | bytes 524288 | tf_op jit(solution)/shard_map/all_to_all | solution.py:335
  22.9 12.1 %collective-permute-start.1 = (bf16[8,64,256]{2,1,0:T(8,128)(2,1)S(1)}, bf16[8,64,256]{2,1,0:T(8,128)(2,1)S(1)}, u32[]{:S(2)}, u32[]{:S(2)}) collective-permute-start(bf16[8,64,256]{2,1,0:T(8,128)(2,1)S(1)} %collective-permute-done.refs_4_), channel_id=1, source_target_pairs={{32,64},{64,96},{96,128},{128,160},{160,192},{192,224},{224,256},{... | collective-permute-start | bytes 786440 | tf_op jit(solution)/shard_map/ppermute | solution.py:336
  25.5 12.1 %collective-permute-start.4 = (bf16[8,64,256]{2,1,0:T(8,128)(2,1)S(1)}, bf16[8,64,256]{2,1,0:T(8,128)(2,1)S(1)}, u32[]{:S(2)}, u32[]{:S(2)}) collective-permute-start(bf16[8,64,256]{2,1,0:T(8,128)(2,1)S(1)} %collective-permute-done.2.refs_5_), channel_id=1, source_target_pairs={{224,192},{256,224},{288,256},{320,288},{352,320},{384,352},{416,3... | collective-permute-start | bytes 786440 | tf_op jit(solution)/shard_map/ppermute | solution.py:337
  35.0 13.1 %collective-permute-start.5 = (bf16[8,64,256]{2,1,0:T(8,128)(2,1)S(1)}, bf16[8,64,256]{2,1,0:T(8,128)(2,1)S(1)}, u32[]{:S(2)}, u32[]{:S(2)}) collective-permute-start(bf16[8,64,256]{2,1,0:T(8,128)(2,1)S(1)} %collective-permute-done.1.refs_7_), channel_id=1, source_target_pairs={{64,96},{96,128},{128,160},{160,192},{192,224},{224,256},{256,288}... | collective-permute-start | bytes 786440 | tf_op jit(solution)/shard_map/ppermute | solution.py:341
  37.6 13.8 %collective-permute-start.6 = (bf16[8,64,256]{2,1,0:T(8,128)(2,1)S(1)}, bf16[8,64,256]{2,1,0:T(8,128)(2,1)S(1)}, u32[]{:S(2)}, u32[]{:S(2)}) collective-permute-start(bf16[8,64,256]{2,1,0:T(8,128)(2,1)S(1)} %collective-permute-done.4.refs_8_), channel_id=1, source_target_pairs={{192,160},{224,192},{256,224},{288,256},{320,288},{352,320},{384,3... | collective-permute-start | bytes 786440 | tf_op jit(solution)/shard_map/ppermute | solution.py:342
  38.9 13.2 %collective-permute-start.3 = (bf16[8,64,256]{2,1,0:T(8,128)(2,1)S(1)}, bf16[8,64,256]{2,1,0:T(8,128)(2,1)S(1)}, u32[]{:S(2)}, u32[]{:S(2)}) collective-permute-start(bf16[8,64,256]{2,1,0:T(8,128)(2,1)S(1)} %prepare_keys.1.kv_ref.refs_3_), channel_id=1, source_target_pairs={{0,256},{32,288},{64,320},{96,352},{128,384},{160,416},{192,448},{... | collective-permute-start | bytes 786440 | tf_op jit(solution)/shard_map/ppermute | solution.py:333
  41.4 24.9 %collective-permute-start.7 = (bf16[32,16,256]{2,1,0:T(8,128)(2,1)S(1)}, bf16[32,16,256]{2,1,0:T(8,128)(2,1)S(1)}, u32[]{:S(2)}, u32[]{:S(2)}) collective-permute-start(bf16[32,16,256]{2,1,0:T(8,128)(2,1)S(1)} %all-to-all-done), channel_id=1, source_target_pairs={{0,0},{1,1},{2,2},{3,3},{4,64},{5,65},{6,66},{7,67},{8,128},{9,129... | collective-permute-start | bytes 786440 | tf_op jit(solution)/shard_map/ppermute | solution.py:343
  48.1 23.6 %collective-permute-start.8 = (bf16[8,64,256]{2,1,0:T(8,128)(2,1)S(1)}, bf16[8,64,256]{2,1,0:T(8,128)(2,1)S(1)}, u32[]{:S(2)}, u32[]{:S(2)}) collective-permute-start(bf16[8,64,256]{2,1,0:T(8,128)(2,1)S(1)} %collective-permute-done.5.refs_9_), channel_id=1, source_target_pairs={{96,128},{128,160},{160,192},{192,224},{352,384},{384,416},{416,44... | collective-permute-start | bytes 786440 | tf_op jit(solution)/shard_map/ppermute | solution.py:344
  51.4 20.4 %collective-permute-start.9 = (bf16[8,64,256]{2,1,0:T(8,128)(2,1)S(1)}, bf16[8,64,256]{2,1,0:T(8,128)(2,1)S(1)}, u32[]{:S(2)}, u32[]{:S(2)}) collective-permute-start(bf16[8,64,256]{2,1,0:T(8,128)(2,1)S(1)} %collective-permute-done.6.refs_10_), channel_id=1, source_target_pairs={{288,256},{320,288},{352,320},{384,352},{289,257},{321,289},{353,3... | collective-permute-start | bytes 786440 | tf_op jit(solution)/shard_map/ppermute | solution.py:345

commit v5 on v4

--- a/solution.py
+++ b/solution.py
@@ -330,7 +330,6 @@
     kv = prepare_keys(where, doc_lengths, key_proj, value_proj, key_gain.reshape(1, HD))
     minus1 = lax.ppermute(kv, "seq", plus_pairs(seqs, 1))
     minus7 = lax.ppermute(kv, "seq", diagonal_pairs(seqs))
-    minus8 = lax.ppermute(kv, "seq", partner_pairs(seqs))
     pages = order_pages(where, kv).reshape(groups, PAGE, 2 * HD)
     mine = lax.all_to_all(pages, "group", split_axis=0, concat_axis=0, tiled=True)
     minus2 = lax.ppermute(minus1, "seq", plus_pairs(seqs, 2))
@@ -341,17 +340,19 @@
     minus3 = lax.ppermute(minus2, "seq", plus_pairs(seqs, 3))
     minus5 = lax.ppermute(minus6, "seq", minus_pairs(seqs, 3))
     cache = lax.ppermute(mine, ("seq", "group"), slot_pairs(seqs, groups))
+    minus3, kv_again = lax.optimization_barrier((minus3, kv))
     plus4 = lax.ppermute(minus3, "seq", plus_pairs(seqs, 4))
     minus4 = lax.ppermute(minus5, "seq", minus_pairs(seqs, 4))
     acc, stat = attend_early(
-        (0, 1, 7, 8, 2, 6, 3, 5),
+        (0, 1, 7, 2, 6, 3, 5),
         where,
         doc_lengths,
         query,
-        [kv, minus1, minus7, minus8, minus2, minus6, minus3, minus5],
-    )
+        [kv, minus1, minus7, minus2, minus6, minus3, minus5],
+    )
+    minus8 = lax.ppermute(kv_again, "seq", partner_pairs(seqs))
     attended, cache = attend_late(
-        (4,), where, doc_lengths, query, acc, stat, cache, [plus4, minus4]
+        (8, 4), where, doc_lengths, query, acc, stat, cache, [minus8, plus4, minus4]
     )
     return attended, cache.reshape(1, 1, groups, 1, PAGE, 2 * HD)
 

time: 75.7 us -> 74.8 us (0.988)
  waiting for transfers between devices: 21 us -> 20 us
    ppermute x1, starting transfers between devices: 6.76 us -> 7.94 us  [body(): cache = lax.ppermute(mine, ('seq', 'group'), slot_pairs(seqs, groups))]
    ppermute x1, waiting for transfers between devices: 5.48 us -> 4.31 us  [body(): plus4 = lax.ppermute(minus3, 'seq', plus_pairs(seqs, 4))]
    ppermute x1, starting transfers between devices: 2.47 us -> 1.31 us  [body(): minus8 = lax.ppermute(kv_again, 'seq', partner_pairs(seqs))]
where the time goes in v5:
time: 74.8 us; the launch traced here: 74.3 us
  starting transfers between devices  39.6 us (53%)
  waiting for transfers between devices  20 us (27%)
  Pallas kernels  13.9 us (19%)
  between operations  0.78 us (1%)
    all_to_all x1, starting transfers between devices, body(): lax.all_to_all(pages, 'group', split_axis=0, concat_axis=0, tiled=True)  11.9 us
    ppermute x1, waiting for transfers between devices, body(): cache = lax.ppermute(mine, ('seq', 'group'), slot_pairs(seqs, groups))  9.85 us
    ppermute x1, starting transfers between devices, body(): cache = lax.ppermute(mine, ('seq', 'group'), slot_pairs(seqs, groups))  7.94 us
    all_to_all x1, waiting for transfers between devices, body(): lax.all_to_all(pages, 'group', split_axis=0, concat_axis=0, tiled=True)  5.83 us
    ppermute x1, starting transfers between devices, body(): minus7 = lax.ppermute(kv, 'seq', diagonal_pairs(seqs))  4.83 us
    pallas_call x1, Pallas kernels, attend_early(): pl.pallas_call(lambda *refs: early_kernel(offsets, *refs), out_shape=(jax...  4.36 us
    ppermute x1, waiting for transfers between devices, body(): plus4 = lax.ppermute(minus3, 'seq', plus_pairs(seqs, 4))  4.31 us
    pallas_call x1, Pallas kernels, attend_late(): pl.pallas_call(lambda *refs: late_kernel(offsets, *refs), out_shape=(jax....  3.73 us
  transfers between devices with their start and end apart: 11, of which 3 were waited for; matrix products, arithmetic and copies ran while one was open for 0% of the time, Pallas kernels for 11%

profile of v5, /device:TPU:42, one launch (start us, length us, event | category | flops | bytes accessed | tf_op | source)
XLA Modules:
  0.0 74.3 jit_solution(17916033836880999421)
XLA Ops:
  0.6 2.2 %prepare_keys.1.kv_ref.refs_3_ = bf16[8,64,256]{2,1,0:T(8,128)(2,1)S(1)} custom-call(s32[1]{0:T(128)} %bitcast.where_ref.refs_0_, s32[1,4]{1,0:T(1,128)} %refs_1_.3, bf16[1,64,1024]{2,1,0:T(8,128)(2,1)} %key_hbm.1, bf16[1,64,1024]{2,1,0:T(8,128)(2,1)} %value_hbm.1, f32[1,128]{1,0:T(1,128)} %bitcast.7), custom_call_target="tpu_custom_call" | custom-call | tf_op jit(solution)/shard_map/prepare_keys/pallas_call | solution.py:82
  2.8 2.6 %collective-permute-start = (bf16[8,64,256]{2,1,0:T(8,128)(2,1)S(1)}, bf16[8,64,256]{2,1,0:T(8,128)(2,1)S(1)}, u32[]{:S(2)}, u32[]{:S(2)}) collective-permute-start(bf16[8,64,256]{2,1,0:T(8,128)(2,1)S(1)} %prepare_keys.1.kv_ref.refs_3_), channel_id=1, source_target_pairs={{0,32},{32,64},{64,96},{96,128},{128,160},{160,192},{192,224},{224... | collective-permute-start | bytes 786440 | tf_op jit(solution)/shard_map/ppermute | solution.py:331
  5.4 4.8 %collective-permute-start.2 = (bf16[8,64,256]{2,1,0:T(8,128)(2,1)S(1)}, bf16[8,64,256]{2,1,0:T(8,128)(2,1)S(1)}, u32[]{:S(2)}, u32[]{:S(2)}) collective-permute-start(bf16[8,64,256]{2,1,0:T(8,128)(2,1)S(1)} %prepare_keys.1.kv_ref.refs_3_), channel_id=1, source_target_pairs={{0,224},{32,256},{64,288},{96,320},{128,352},{160,384},{192,416},{... | collective-permute-start | bytes 786440 | tf_op jit(solution)/shard_map/ppermute | solution.py:332
  10.2 0.7 order_pages.1
  11.0 11.9 %all-to-all-start = ((bf16[32,16,256]{2,1,0:T(8,128)(2,1)}), bf16[32,16,256]{2,1,0:T(8,128)(2,1)S(1)}, u32[]{:S(2)}, u32[]{:S(2)}) async-start(bf16[32,16,256]{2,1,0:T(8,128)(2,1)} %bitcast.3), calls=%async_computation | async-start | bytes 524288 | tf_op jit(solution)/shard_map/all_to_all | solution.py:334
  22.9 0.0 collective-permute-done.refs_4_
  22.9 2.6 %collective-permute-start.1 = (bf16[8,64,256]{2,1,0:T(8,128)(2,1)S(1)}, bf16[8,64,256]{2,1,0:T(8,128)(2,1)S(1)}, u32[]{:S(2)}, u32[]{:S(2)}) collective-permute-start(bf16[8,64,256]{2,1,0:T(8,128)(2,1)S(1)} %collective-permute-done.refs_4_), channel_id=1, source_target_pairs={{32,64},{64,96},{96,128},{128,160},{160,192},{192,224},{224,256},{... | collective-permute-start | bytes 786440 | tf_op jit(solution)/shard_map/ppermute | solution.py:335
  25.5 0.0 collective-permute-done.2.refs_5_
  25.5 0.7 collective-permute-start.3
  26.2 2.9 %prepare_queries.1.refs_2_ = bf16[8,128,512]{2,1,0:T(8,128)(2,1)S(1)} custom-call(s32[1]{0:T(128)} %bitcast.where_ref.refs_0_, s32[1,4]{1,0:T(1,128)} %refs_1_.3, bf16[1,64,8192]{2,1,0:T(8,128)(2,1)} %query_hbm.1, f32[1,128]{1,0:T(1,128)} %bitcast.8), custom_call_target="tpu_custom_call" | custom-call | flops 10000000 | bytes 4194304 | tf_op jit(solution)/shard_map/prepare_queries/pallas_call | solution.py:133
  29.2 5.8 %all-to-all-done = bf16[32,16,256]{2,1,0:T(8,128)(2,1)S(1)} async-done(((bf16[32,16,256]{2,1,0:T(8,128)(2,1)}), bf16[32,16,256]{2,1,0:T(8,128)(2,1)S(1)}, u32[]{:S(2)}, u32[]{:S(2)}) %all-to-all-start) | async-done | bytes 262176 | tf_op jit(solution)/shard_map/all_to_all | solution.py:334
  35.0 0.0 collective-permute-done.1.refs_6_
  35.0 2.6 %collective-permute-start.4 = (bf16[8,64,256]{2,1,0:T(8,128)(2,1)S(1)}, bf16[8,64,256]{2,1,0:T(8,128)(2,1)S(1)}, u32[]{:S(2)}, u32[]{:S(2)}) collective-permute-start(bf16[8,64,256]{2,1,0:T(8,128)(2,1)S(1)} %collective-permute-done.1.refs_6_), channel_id=1, source_target_pairs={{64,96},{96,128},{128,160},{160,192},{192,224},{224,256},{256,288}... | collective-permute-start | bytes 786440 | tf_op jit(solution)/shard_map/ppermute | solution.py:340
  37.6 0.0 collective-permute-done.3.refs_7_
  37.6 1.3 %collective-permute-start.5 = (bf16[8,64,256]{2,1,0:T(8,128)(2,1)S(1)}, bf16[8,64,256]{2,1,0:T(8,128)(2,1)S(1)}, u32[]{:S(2)}, u32[]{:S(2)}) collective-permute-start(bf16[8,64,256]{2,1,0:T(8,128)(2,1)S(1)} %collective-permute-done.3.refs_7_), channel_id=1, source_target_pairs={{192,160},{224,192},{256,224},{288,256},{320,288},{352,320},{384,3... | collective-permute-start | bytes 786440 | tf_op jit(solution)/shard_map/ppermute | solution.py:341
  38.9 7.9 %collective-permute-start.6 = (bf16[32,16,256]{2,1,0:T(8,128)(2,1)S(1)}, bf16[32,16,256]{2,1,0:T(8,128)(2,1)S(1)}, u32[]{:S(2)}, u32[]{:S(2)}) collective-permute-start(bf16[32,16,256]{2,1,0:T(8,128)(2,1)S(1)} %all-to-all-done), channel_id=1, source_target_pairs={{0,0},{1,1},{2,2},{3,3},{4,64},{5,65},{6,66},{7,67},{8,128},{9,129... | collective-permute-start | bytes 786440 | tf_op jit(solution)/shard_map/ppermute | solution.py:342
  46.8 0.0 collective-permute-done.4.refs_8_
  46.8 3.2 %collective-permute-start.8 = (bf16[8,64,256]{2,1,0:T(8,128)(2,1)S(1)}, bf16[8,64,256]{2,1,0:T(8,128)(2,1)S(1)}, u32[]{:S(2)}, u32[]{:S(2)}) collective-permute-start(bf16[8,64,256]{2,1,0:T(8,128)(2,1)S(1)} %collective-permute-done.4.refs_8_), channel_id=1, source_target_pairs={{96,128},{128,160},{160,192},{192,224},{352,384},{384,416},{416,44... | collective-permute-start | bytes 786440 | tf_op jit(solution)/shard_map/ppermute | solution.py:344
  50.1 1.3 %collective-permute-start.7 = (bf16[8,64,256]{2,1,0:T(8,128)(2,1)S(1)}, bf16[8,64,256]{2,1,0:T(8,128)(2,1)S(1)}, u32[]{:S(2)}, u32[]{:S(2)}) collective-permute-start(bf16[8,64,256]{2,1,0:T(8,128)(2,1)S(1)} %prepare_keys.1.kv_ref.refs_3_), channel_id=1, source_target_pairs={{0,256},{32,288},{64,320},{96,352},{128,384},{160,416},{192,448},{... | collective-permute-start | bytes 786440 | tf_op jit(solution)/shard_map/ppermute | solution.py:353
  51.4 0.0 collective-permute-done.5.refs_9_
  51.4 0.7 collective-permute-start.9
  52.1 4.4 %attend_early.1 = (f32[8,128,512]{2,1,0:T(8,128)S(1)}, f32[8,8,512]{2,1,0:T(8,128)S(1)}) custom-call(s32[1]{0:T(128)} %bitcast.where_ref.refs_0_, s32[1,4]{1,0:T(1,128)} %refs_1_.3, bf16[8,128,512]{2,1,0:T(8,128)(2,1)S(1)} %prepare_queries.1.refs_2_, bf16[8,64,256]{2,1,0:T(8,128)(2,1)S(1)} %prepare_keys.1.kv_ref.refs_3_, ...), custom_call_target="tpu_custom_call" | custom-call | flops 939524096 | bytes 4194304 | tf_op jit(solution)/shard_map/attend_early/pallas_call | solution.py:238
  56.4 9.9 %collective-permute-done.6.refs_5_ = bf16[32,16,256]{2,1,0:T(8,128)(2,1)S(1)} collective-permute-done((bf16[32,16,256]{2,1,0:T(8,128)(2,1)S(1)}, bf16[32,16,256]{2,1,0:T(8,128)(2,1)S(1)}, u32[]{:S(2)}, u32[]{:S(2)}) %collective-permute-start.6) | collective-permute-done | bytes 262176 | tf_op jit(solution)/shard_map/ppermute | solution.py:342
  66.3 4.3 %collective-permute-done.8.refs_7_ = bf16[8,64,256]{2,1,0:T(8,128)(2,1)S(1)} collective-permute-done((bf16[8,64,256]{2,1,0:T(8,128)(2,1)S(1)}, bf16[8,64,256]{2,1,0:T(8,128)(2,1)S(1)}, u32[]{:S(2)}, u32[]{:S(2)}) %collective-permute-start.8) | collective-permute-done | bytes 262176 | tf_op jit(solution)/shard_map/ppermute | solution.py:344
  70.6 0.0 collective-permute-done.7.refs_6_
  70.6 0.0 collective-permute-done.9.refs_8_
  70.6 3.7 %attend_late.1 = (bf16[1,64,8192]{2,1,0:T(8,128)(2,1)}, bf16[32,16,256]{2,1,0:T(8,128)(2,1)}) custom-call(s32[1]{0:T(128)} %bitcast.where_ref.refs_0_, s32[1,4]{1,0:T(1,128)} %refs_1_.3, bf16[8,128,512]{2,1,0:T(8,128)(2,1)S(1)} %prepare_queries.1.refs_2_, f32[8,128,512]{2,1,0:T(8,128)S(1)} %get-tuple-element.18.refs_3_, ...), custom_call_target="tpu_custom_call" | custom-call | flops 268435456 | bytes 4194304 | tf_op jit(solution)/shard_map/attend_late/pallas_call | solution.py:254
Async XLA Ops:
  2.8 20.1 %collective-permute-start = (bf16[8,64,256]{2,1,0:T(8,128)(2,1)S(1)}, bf16[8,64,256]{2,1,0:T(8,128)(2,1)S(1)}, u32[]{:S(2)}, u32[]{:S(2)}) collective-permute-start(bf16[8,64,256]{2,1,0:T(8,128)(2,1)S(1)} %prepare_keys.1.kv_ref.refs_3_), channel_id=1, source_target_pairs={{0,32},{32,64},{64,96},{96,128},{128,160},{160,192},{192,224},{224... | collective-permute-start | bytes 786440 | tf_op jit(solution)/shard_map/ppermute | solution.py:331
  5.4 20.1 %collective-permute-start.2 = (bf16[8,64,256]{2,1,0:T(8,128)(2,1)S(1)}, bf16[8,64,256]{2,1,0:T(8,128)(2,1)S(1)}, u32[]{:S(2)}, u32[]{:S(2)}) collective-permute-start(bf16[8,64,256]{2,1,0:T(8,128)(2,1)S(1)} %prepare_keys.1.kv_ref.refs_3_), channel_id=1, source_target_pairs={{0,224},{32,256},{64,288},{96,320},{128,352},{160,384},{192,416},{... | collective-permute-start | bytes 786440 | tf_op jit(solution)/shard_map/ppermute | solution.py:332
  11.0 24.0 %all-to-all-start = ((bf16[32,16,256]{2,1,0:T(8,128)(2,1)}), bf16[32,16,256]{2,1,0:T(8,128)(2,1)S(1)}, u32[]{:S(2)}, u32[]{:S(2)}) async-start(bf16[32,16,256]{2,1,0:T(8,128)(2,1)} %bitcast.3), calls=%async_computation | async-start | bytes 524288 | tf_op jit(solution)/shard_map/all_to_all | solution.py:334
  22.9 12.1 %collective-permute-start.1 = (bf16[8,64,256]{2,1,0:T(8,128)(2,1)S(1)}, bf16[8,64,256]{2,1,0:T(8,128)(2,1)S(1)}, u32[]{:S(2)}, u32[]{:S(2)}) collective-permute-start(bf16[8,64,256]{2,1,0:T(8,128)(2,1)S(1)} %collective-permute-done.refs_4_), channel_id=1, source_target_pairs={{32,64},{64,96},{96,128},{128,160},{160,192},{192,224},{224,256},{... | collective-permute-start | bytes 786440 | tf_op jit(solution)/shard_map/ppermute | solution.py:335
  25.5 12.1 %collective-permute-start.3 = (bf16[8,64,256]{2,1,0:T(8,128)(2,1)S(1)}, bf16[8,64,256]{2,1,0:T(8,128)(2,1)S(1)}, u32[]{:S(2)}, u32[]{:S(2)}) collective-permute-start(bf16[8,64,256]{2,1,0:T(8,128)(2,1)S(1)} %collective-permute-done.2.refs_5_), channel_id=1, source_target_pairs={{224,192},{256,224},{288,256},{320,288},{352,320},{384,352},{416,3... | collective-permute-start | bytes 786440 | tf_op jit(solution)/shard_map/ppermute | solution.py:336
  35.0 11.8 %collective-permute-start.4 = (bf16[8,64,256]{2,1,0:T(8,128)(2,1)S(1)}, bf16[8,64,256]{2,1,0:T(8,128)(2,1)S(1)}, u32[]{:S(2)}, u32[]{:S(2)}) collective-permute-start(bf16[8,64,256]{2,1,0:T(8,128)(2,1)S(1)} %collective-permute-done.1.refs_6_), channel_id=1, source_target_pairs={{64,96},{96,128},{128,160},{160,192},{192,224},{224,256},{256,288}... | collective-permute-start | bytes 786440 | tf_op jit(solution)/shard_map/ppermute | solution.py:340
  37.6 13.8 %collective-permute-start.5 = (bf16[8,64,256]{2,1,0:T(8,128)(2,1)S(1)}, bf16[8,64,256]{2,1,0:T(8,128)(2,1)S(1)}, u32[]{:S(2)}, u32[]{:S(2)}) collective-permute-start(bf16[8,64,256]{2,1,0:T(8,128)(2,1)S(1)} %collective-permute-done.3.refs_7_), channel_id=1, source_target_pairs={{192,160},{224,192},{256,224},{288,256},{320,288},{352,320},{384,3... | collective-permute-start | bytes 786440 | tf_op jit(solution)/shard_map/ppermute | solution.py:341
  38.9 27.4 %collective-permute-start.6 = (bf16[32,16,256]{2,1,0:T(8,128)(2,1)S(1)}, bf16[32,16,256]{2,1,0:T(8,128)(2,1)S(1)}, u32[]{:S(2)}, u32[]{:S(2)}) collective-permute-start(bf16[32,16,256]{2,1,0:T(8,128)(2,1)S(1)} %all-to-all-done), channel_id=1, source_target_pairs={{0,0},{1,1},{2,2},{3,3},{4,64},{5,65},{6,66},{7,67},{8,128},{9,129... | collective-permute-start | bytes 786440 | tf_op jit(solution)/shard_map/ppermute | solution.py:342
  46.8 23.8 %collective-permute-start.8 = (bf16[8,64,256]{2,1,0:T(8,128)(2,1)S(1)}, bf16[8,64,256]{2,1,0:T(8,128)(2,1)S(1)}, u32[]{:S(2)}, u32[]{:S(2)}) collective-permute-start(bf16[8,64,256]{2,1,0:T(8,128)(2,1)S(1)} %collective-permute-done.4.refs_8_), channel_id=1, source_target_pairs={{96,128},{128,160},{160,192},{192,224},{352,384},{384,416},{416,44... | collective-permute-start | bytes 786440 | tf_op jit(solution)/shard_map/ppermute | solution.py:344
  50.1 20.5 %collective-permute-start.7 = (bf16[8,64,256]{2,1,0:T(8,128)(2,1)S(1)}, bf16[8,64,256]{2,1,0:T(8,128)(2,1)S(1)}, u32[]{:S(2)}, u32[]{:S(2)}) collective-permute-start(bf16[8,64,256]{2,1,0:T(8,128)(2,1)S(1)} %prepare_keys.1.kv_ref.refs_3_), channel_id=1, source_target_pairs={{0,256},{32,288},{64,320},{96,352},{128,384},{160,416},{192,448},{... | collective-permute-start | bytes 786440 | tf_op jit(solution)/shard_map/ppermute | solution.py:353
  51.4 19.2 %collective-permute-start.9 = (bf16[8,64,256]{2,1,0:T(8,128)(2,1)S(1)}, bf16[8,64,256]{2,1,0:T(8,128)(2,1)S(1)}, u32[]{:S(2)}, u32[]{:S(2)}) collective-permute-start(bf16[8,64,256]{2,1,0:T(8,128)(2,1)S(1)} %collective-permute-done.5.refs_9_), channel_id=1, source_target_pairs={{288,256},{320,288},{352,320},{384,352},{289,257},{321,289},{353,3... | collective-permute-start | bytes 786440 | tf_op jit(solution)/shard_map/ppermute | solution.py:345

commit v6 on v5

--- a/solution.py
+++ b/solution.py
@@ -35,12 +35,16 @@
 
 
 def key_kernel(
-    where_ref, lens_ref, key_hbm, value_hbm, gain_hbm, kv_ref, key_ref, value_ref, gain_ref, sems
+    where_ref, lens_ref, key_hbm, value_hbm, gain_hbm, kv_ref, key_ref, gain_ref, sems
 ):
     copies = [
         pltpu.make_async_copy(key_hbm.at[0], key_ref, sems.at[0]),
         pltpu.make_async_copy(gain_hbm, gain_ref, sems.at[1]),
-        pltpu.make_async_copy(value_hbm.at[0], value_ref, sems.at[2]),
+    ] + [
+        pltpu.make_async_copy(
+            value_hbm.at[0, :, pl.ds(h * HD, HD)], kv_ref.at[h, :, pl.ds(HD, HD)], sems.at[2 + h]
+        )
+        for h in range(KVH)
     ]
     for copy in copies:
         copy.start()
@@ -63,9 +67,8 @@
         normed = values_f * inv_rms * gain
         swapped = pltpu.roll(normed, half, 1)
         kv_ref[h, :, :HD] = (normed * cosine + swapped * sine).astype(jnp.bfloat16)
-    copies[2].wait()
-    for h in range(KVH):
-        kv_ref[h, :, HD:] = value_ref[:, pl.ds(h * HD, HD)]
+    for copy in copies[2:]:
+        copy.wait()
 
 
 SMEM_SPEC = pl.BlockSpec(memory_space=pltpu.SMEM)
@@ -86,9 +89,8 @@
         out_specs=VMEM_SPEC,
         scratch_shapes=[
             pltpu.VMEM((ROWS, KVH * HD), jnp.bfloat16),
-            pltpu.VMEM((ROWS, KVH * HD), jnp.bfloat16),
             pltpu.VMEM((1, HD), jnp.float32),
-            pltpu.SemaphoreType.DMA((3,)),
+            pltpu.SemaphoreType.DMA((2 + KVH,)),
         ],
         compiler_params=PARAMS,
         name="prepare_keys",

time: 74.8 us -> 74.9 us (level)
  no operation moved by 1% of the time
where the time goes in v6:
time: 74.9 us; the launch traced here: 74.4 us
  starting transfers between devices  39.6 us (53%)
  waiting for transfers between devices  20 us (27%)
  Pallas kernels  14 us (19%)
  between operations  0.78 us (1%)
    all_to_all x1, starting transfers between devices, body(): lax.all_to_all(pages, 'group', split_axis=0, concat_axis=0, tiled=True)  11.9 us
    ppermute x1, waiting for transfers between devices, body(): cache = lax.ppermute(mine, ('seq', 'group'), slot_pairs(seqs, groups))  9.85 us
    ppermute x1, starting transfers between devices, body(): cache = lax.ppermute(mine, ('seq', 'group'), slot_pairs(seqs, groups))  7.94 us
    all_to_all x1, waiting for transfers between devices, body(): lax.all_to_all(pages, 'group', split_axis=0, concat_axis=0, tiled=True)  5.83 us
    ppermute x1, starting transfers between devices, body(): minus7 = lax.ppermute(kv, 'seq', diagonal_pairs(seqs))  4.83 us
    pallas_call x1, Pallas kernels, attend_early(): pl.pallas_call(lambda *refs: early_kernel(offsets, *refs), out_shape=(jax...  4.36 us
    ppermute x1, waiting for transfers between devices, body(): plus4 = lax.ppermute(minus3, 'seq', plus_pairs(seqs, 4))  4.31 us
    pallas_call x1, Pallas kernels, attend_late(): pl.pallas_call(lambda *refs: late_kernel(offsets, *refs), out_shape=(jax....  3.73 us
  transfers between devices with their start and end apart: 11, of which 3 were waited for; matrix products, arithmetic and copies ran while one was open for 0% of the time, Pallas kernels for 11%

profile of v6, /device:TPU:42, one launch (start us, length us, event | category | flops | bytes accessed | tf_op | source)
XLA Modules:
  0.0 74.4 jit_solution(6588319384700816770)
XLA Ops:
  0.6 2.2 %prepare_keys.1.kv_ref.refs_3_ = bf16[8,64,256]{2,1,0:T(8,128)(2,1)S(1)} custom-call(s32[1]{0:T(128)} %bitcast.where_ref.refs_0_, s32[1,4]{1,0:T(1,128)} %refs_1_.3, bf16[1,64,1024]{2,1,0:T(8,128)(2,1)} %key_hbm.1, bf16[1,64,1024]{2,1,0:T(8,128)(2,1)} %value_hbm.1, f32[1,128]{1,0:T(1,128)} %bitcast.7), custom_call_target="tpu_custom_call" | custom-call | tf_op jit(solution)/shard_map/prepare_keys/pallas_call | solution.py:85
  2.9 2.6 %collective-permute-start = (bf16[8,64,256]{2,1,0:T(8,128)(2,1)S(1)}, bf16[8,64,256]{2,1,0:T(8,128)(2,1)S(1)}, u32[]{:S(2)}, u32[]{:S(2)}) collective-permute-start(bf16[8,64,256]{2,1,0:T(8,128)(2,1)S(1)} %prepare_keys.1.kv_ref.refs_3_), channel_id=1, source_target_pairs={{0,32},{32,64},{64,96},{96,128},{128,160},{160,192},{192,224},{224... | collective-permute-start | bytes 786440 | tf_op jit(solution)/shard_map/ppermute | solution.py:333
  5.5 4.8 %collective-permute-start.2 = (bf16[8,64,256]{2,1,0:T(8,128)(2,1)S(1)}, bf16[8,64,256]{2,1,0:T(8,128)(2,1)S(1)}, u32[]{:S(2)}, u32[]{:S(2)}) collective-permute-start(bf16[8,64,256]{2,1,0:T(8,128)(2,1)S(1)} %prepare_keys.1.kv_ref.refs_3_), channel_id=1, source_target_pairs={{0,224},{32,256},{64,288},{96,320},{128,352},{160,384},{192,416},{... | collective-permute-start | bytes 786440 | tf_op jit(solution)/shard_map/ppermute | solution.py:334
  10.3 0.7 order_pages.1
  11.0 11.9 %all-to-all-start = ((bf16[32,16,256]{2,1,0:T(8,128)(2,1)}), bf16[32,16,256]{2,1,0:T(8,128)(2,1)S(1)}, u32[]{:S(2)}, u32[]{:S(2)}) async-start(bf16[32,16,256]{2,1,0:T(8,128)(2,1)} %bitcast.3), calls=%async_computation | async-start | bytes 524288 | tf_op jit(solution)/shard_map/all_to_all | solution.py:336
  23.0 0.0 collective-permute-done.refs_4_
  23.0 2.6 %collective-permute-start.1 = (bf16[8,64,256]{2,1,0:T(8,128)(2,1)S(1)}, bf16[8,64,256]{2,1,0:T(8,128)(2,1)S(1)}, u32[]{:S(2)}, u32[]{:S(2)}) collective-permute-start(bf16[8,64,256]{2,1,0:T(8,128)(2,1)S(1)} %collective-permute-done.refs_4_), channel_id=1, source_target_pairs={{32,64},{64,96},{96,128},{128,160},{160,192},{192,224},{224,256},{... | collective-permute-start | bytes 786440 | tf_op jit(solution)/shard_map/ppermute | solution.py:337
  25.6 0.0 collective-permute-done.2.refs_5_
  25.6 0.7 collective-permute-start.3
  26.3 2.9 %prepare_queries.1.refs_2_ = bf16[8,128,512]{2,1,0:T(8,128)(2,1)S(1)} custom-call(s32[1]{0:T(128)} %bitcast.where_ref.refs_0_, s32[1,4]{1,0:T(1,128)} %refs_1_.3, bf16[1,64,8192]{2,1,0:T(8,128)(2,1)} %query_hbm.1, f32[1,128]{1,0:T(1,128)} %bitcast.8), custom_call_target="tpu_custom_call" | custom-call | flops 10000000 | bytes 4194304 | tf_op jit(solution)/shard_map/prepare_queries/pallas_call | solution.py:135
  29.2 5.8 %all-to-all-done = bf16[32,16,256]{2,1,0:T(8,128)(2,1)S(1)} async-done(((bf16[32,16,256]{2,1,0:T(8,128)(2,1)}), bf16[32,16,256]{2,1,0:T(8,128)(2,1)S(1)}, u32[]{:S(2)}, u32[]{:S(2)}) %all-to-all-start) | async-done | bytes 262176 | tf_op jit(solution)/shard_map/all_to_all | solution.py:336
  35.0 0.0 collective-permute-done.1.refs_6_
  35.0 2.6 %collective-permute-start.4 = (bf16[8,64,256]{2,1,0:T(8,128)(2,1)S(1)}, bf16[8,64,256]{2,1,0:T(8,128)(2,1)S(1)}, u32[]{:S(2)}, u32[]{:S(2)}) collective-permute-start(bf16[8,64,256]{2,1,0:T(8,128)(2,1)S(1)} %collective-permute-done.1.refs_6_), channel_id=1, source_target_pairs={{64,96},{96,128},{128,160},{160,192},{192,224},{224,256},{256,288}... | collective-permute-start | bytes 786440 | tf_op jit(solution)/shard_map/ppermute | solution.py:342
  37.6 0.0 collective-permute-done.3.refs_7_
  37.6 1.3 %collective-permute-start.5 = (bf16[8,64,256]{2,1,0:T(8,128)(2,1)S(1)}, bf16[8,64,256]{2,1,0:T(8,128)(2,1)S(1)}, u32[]{:S(2)}, u32[]{:S(2)}) collective-permute-start(bf16[8,64,256]{2,1,0:T(8,128)(2,1)S(1)} %collective-permute-done.3.refs_7_), channel_id=1, source_target_pairs={{192,160},{224,192},{256,224},{288,256},{320,288},{352,320},{384,3... | collective-permute-start | bytes 786440 | tf_op jit(solution)/shard_map/ppermute | solution.py:343
  38.9 7.9 %collective-permute-start.6 = (bf16[32,16,256]{2,1,0:T(8,128)(2,1)S(1)}, bf16[32,16,256]{2,1,0:T(8,128)(2,1)S(1)}, u32[]{:S(2)}, u32[]{:S(2)}) collective-permute-start(bf16[32,16,256]{2,1,0:T(8,128)(2,1)S(1)} %all-to-all-done), channel_id=1, source_target_pairs={{0,0},{1,1},{2,2},{3,3},{4,64},{5,65},{6,66},{7,67},{8,128},{9,129... | collective-permute-start | bytes 786440 | tf_op jit(solution)/shard_map/ppermute | solution.py:344
  46.9 0.0 collective-permute-done.4.refs_8_
  46.9 3.2 %collective-permute-start.8 = (bf16[8,64,256]{2,1,0:T(8,128)(2,1)S(1)}, bf16[8,64,256]{2,1,0:T(8,128)(2,1)S(1)}, u32[]{:S(2)}, u32[]{:S(2)}) collective-permute-start(bf16[8,64,256]{2,1,0:T(8,128)(2,1)S(1)} %collective-permute-done.4.refs_8_), channel_id=1, source_target_pairs={{96,128},{128,160},{160,192},{192,224},{352,384},{384,416},{416,44... | collective-permute-start | bytes 786440 | tf_op jit(solution)/shard_map/ppermute | solution.py:346
  50.1 1.3 %collective-permute-start.7 = (bf16[8,64,256]{2,1,0:T(8,128)(2,1)S(1)}, bf16[8,64,256]{2,1,0:T(8,128)(2,1)S(1)}, u32[]{:S(2)}, u32[]{:S(2)}) collective-permute-start(bf16[8,64,256]{2,1,0:T(8,128)(2,1)S(1)} %prepare_keys.1.kv_ref.refs_3_), channel_id=1, source_target_pairs={{0,256},{32,288},{64,320},{96,352},{128,384},{160,416},{192,448},{... | collective-permute-start | bytes 786440 | tf_op jit(solution)/shard_map/ppermute | solution.py:355
  51.4 0.0 collective-permute-done.5.refs_9_
  51.4 0.7 collective-permute-start.9
  52.1 4.4 %attend_early.1 = (f32[8,128,512]{2,1,0:T(8,128)S(1)}, f32[8,8,512]{2,1,0:T(8,128)S(1)}) custom-call(s32[1]{0:T(128)} %bitcast.where_ref.refs_0_, s32[1,4]{1,0:T(1,128)} %refs_1_.3, bf16[8,128,512]{2,1,0:T(8,128)(2,1)S(1)} %prepare_queries.1.refs_2_, bf16[8,64,256]{2,1,0:T(8,128)(2,1)S(1)} %prepare_keys.1.kv_ref.refs_3_, ...), custom_call_target="tpu_custom_call" | custom-call | flops 939524096 | bytes 4194304 | tf_op jit(solution)/shard_map/attend_early/pallas_call | solution.py:240
  56.5 9.9 %collective-permute-done.6.refs_5_ = bf16[32,16,256]{2,1,0:T(8,128)(2,1)S(1)} collective-permute-done((bf16[32,16,256]{2,1,0:T(8,128)(2,1)S(1)}, bf16[32,16,256]{2,1,0:T(8,128)(2,1)S(1)}, u32[]{:S(2)}, u32[]{:S(2)}) %collective-permute-start.6) | collective-permute-done | bytes 262176 | tf_op jit(solution)/shard_map/ppermute | solution.py:344
  66.3 4.3 %collective-permute-done.8.refs_7_ = bf16[8,64,256]{2,1,0:T(8,128)(2,1)S(1)} collective-permute-done((bf16[8,64,256]{2,1,0:T(8,128)(2,1)S(1)}, bf16[8,64,256]{2,1,0:T(8,128)(2,1)S(1)}, u32[]{:S(2)}, u32[]{:S(2)}) %collective-permute-start.8) | collective-permute-done | bytes 262176 | tf_op jit(solution)/shard_map/ppermute | solution.py:346
  70.6 0.0 collective-permute-done.7.refs_6_
  70.6 0.0 collective-permute-done.9.refs_8_
  70.7 3.7 %attend_late.1 = (bf16[1,64,8192]{2,1,0:T(8,128)(2,1)}, bf16[32,16,256]{2,1,0:T(8,128)(2,1)}) custom-call(s32[1]{0:T(128)} %bitcast.where_ref.refs_0_, s32[1,4]{1,0:T(1,128)} %refs_1_.3, bf16[8,128,512]{2,1,0:T(8,128)(2,1)S(1)} %prepare_queries.1.refs_2_, f32[8,128,512]{2,1,0:T(8,128)S(1)} %get-tuple-element.18.refs_3_, ...), custom_call_target="tpu_custom_call" | custom-call | flops 268435456 | bytes 4194304 | tf_op jit(solution)/shard_map/attend_late/pallas_call | solution.py:256
Async XLA Ops:
  2.9 20.1 %collective-permute-start = (bf16[8,64,256]{2,1,0:T(8,128)(2,1)S(1)}, bf16[8,64,256]{2,1,0:T(8,128)(2,1)S(1)}, u32[]{:S(2)}, u32[]{:S(2)}) collective-permute-start(bf16[8,64,256]{2,1,0:T(8,128)(2,1)S(1)} %prepare_keys.1.kv_ref.refs_3_), channel_id=1, source_target_pairs={{0,32},{32,64},{64,96},{96,128},{128,160},{160,192},{192,224},{224... | collective-permute-start | bytes 786440 | tf_op jit(solution)/shard_map/ppermute | solution.py:333
  5.5 20.1 %collective-permute-start.2 = (bf16[8,64,256]{2,1,0:T(8,128)(2,1)S(1)}, bf16[8,64,256]{2,1,0:T(8,128)(2,1)S(1)}, u32[]{:S(2)}, u32[]{:S(2)}) collective-permute-start(bf16[8,64,256]{2,1,0:T(8,128)(2,1)S(1)} %prepare_keys.1.kv_ref.refs_3_), channel_id=1, source_target_pairs={{0,224},{32,256},{64,288},{96,320},{128,352},{160,384},{192,416},{... | collective-permute-start | bytes 786440 | tf_op jit(solution)/shard_map/ppermute | solution.py:334
  11.0 24.0 %all-to-all-start = ((bf16[32,16,256]{2,1,0:T(8,128)(2,1)}), bf16[32,16,256]{2,1,0:T(8,128)(2,1)S(1)}, u32[]{:S(2)}, u32[]{:S(2)}) async-start(bf16[32,16,256]{2,1,0:T(8,128)(2,1)} %bitcast.3), calls=%async_computation | async-start | bytes 524288 | tf_op jit(solution)/shard_map/all_to_all | solution.py:336
  23.0 12.1 %collective-permute-start.1 = (bf16[8,64,256]{2,1,0:T(8,128)(2,1)S(1)}, bf16[8,64,256]{2,1,0:T(8,128)(2,1)S(1)}, u32[]{:S(2)}, u32[]{:S(2)}) collective-permute-start(bf16[8,64,256]{2,1,0:T(8,128)(2,1)S(1)} %collective-permute-done.refs_4_), channel_id=1, source_target_pairs={{32,64},{64,96},{96,128},{128,160},{160,192},{192,224},{224,256},{... | collective-permute-start | bytes 786440 | tf_op jit(solution)/shard_map/ppermute | solution.py:337
  25.6 12.1 %collective-permute-start.3 = (bf16[8,64,256]{2,1,0:T(8,128)(2,1)S(1)}, bf16[8,64,256]{2,1,0:T(8,128)(2,1)S(1)}, u32[]{:S(2)}, u32[]{:S(2)}) collective-permute-start(bf16[8,64,256]{2,1,0:T(8,128)(2,1)S(1)} %collective-permute-done.2.refs_5_), channel_id=1, source_target_pairs={{224,192},{256,224},{288,256},{320,288},{352,320},{384,352},{416,3... | collective-permute-start | bytes 786440 | tf_op jit(solution)/shard_map/ppermute | solution.py:338
  35.0 11.8 %collective-permute-start.4 = (bf16[8,64,256]{2,1,0:T(8,128)(2,1)S(1)}, bf16[8,64,256]{2,1,0:T(8,128)(2,1)S(1)}, u32[]{:S(2)}, u32[]{:S(2)}) collective-permute-start(bf16[8,64,256]{2,1,0:T(8,128)(2,1)S(1)} %collective-permute-done.1.refs_6_), channel_id=1, source_target_pairs={{64,96},{96,128},{128,160},{160,192},{192,224},{224,256},{256,288}... | collective-permute-start | bytes 786440 | tf_op jit(solution)/shard_map/ppermute | solution.py:342
  37.6 13.8 %collective-permute-start.5 = (bf16[8,64,256]{2,1,0:T(8,128)(2,1)S(1)}, bf16[8,64,256]{2,1,0:T(8,128)(2,1)S(1)}, u32[]{:S(2)}, u32[]{:S(2)}) collective-permute-start(bf16[8,64,256]{2,1,0:T(8,128)(2,1)S(1)} %collective-permute-done.3.refs_7_), channel_id=1, source_target_pairs={{192,160},{224,192},{256,224},{288,256},{320,288},{352,320},{384,3... | collective-permute-start | bytes 786440 | tf_op jit(solution)/shard_map/ppermute | solution.py:343
  38.9 27.4 %collective-permute-start.6 = (bf16[32,16,256]{2,1,0:T(8,128)(2,1)S(1)}, bf16[32,16,256]{2,1,0:T(8,128)(2,1)S(1)}, u32[]{:S(2)}, u32[]{:S(2)}) collective-permute-start(bf16[32,16,256]{2,1,0:T(8,128)(2,1)S(1)} %all-to-all-done), channel_id=1, source_target_pairs={{0,0},{1,1},{2,2},{3,3},{4,64},{5,65},{6,66},{7,67},{8,128},{9,129... | collective-permute-start | bytes 786440 | tf_op jit(solution)/shard_map/ppermute | solution.py:344
  46.9 23.8 %collective-permute-start.8 = (bf16[8,64,256]{2,1,0:T(8,128)(2,1)S(1)}, bf16[8,64,256]{2,1,0:T(8,128)(2,1)S(1)}, u32[]{:S(2)}, u32[]{:S(2)}) collective-permute-start(bf16[8,64,256]{2,1,0:T(8,128)(2,1)S(1)} %collective-permute-done.4.refs_8_), channel_id=1, source_target_pairs={{96,128},{128,160},{160,192},{192,224},{352,384},{384,416},{416,44... | collective-permute-start | bytes 786440 | tf_op jit(solution)/shard_map/ppermute | solution.py:346
  50.1 20.5 %collective-permute-start.7 = (bf16[8,64,256]{2,1,0:T(8,128)(2,1)S(1)}, bf16[8,64,256]{2,1,0:T(8,128)(2,1)S(1)}, u32[]{:S(2)}, u32[]{:S(2)}) collective-permute-start(bf16[8,64,256]{2,1,0:T(8,128)(2,1)S(1)} %prepare_keys.1.kv_ref.refs_3_), channel_id=1, source_target_pairs={{0,256},{32,288},{64,320},{96,352},{128,384},{160,416},{192,448},{... | collective-permute-start | bytes 786440 | tf_op jit(solution)/shard_map/ppermute | solution.py:355
  51.4 19.2 %collective-permute-start.9 = (bf16[8,64,256]{2,1,0:T(8,128)(2,1)S(1)}, bf16[8,64,256]{2,1,0:T(8,128)(2,1)S(1)}, u32[]{:S(2)}, u32[]{:S(2)}) collective-permute-start(bf16[8,64,256]{2,1,0:T(8,128)(2,1)S(1)} %collective-permute-done.5.refs_9_), channel_id=1, source_target_pairs={{288,256},{320,288},{352,320},{384,352},{289,257},{321,289},{353,3... | collective-permute-start | bytes 786440 | tf_op jit(solution)/shard_map/ppermute | solution.py:347
